TPU v7x, 256 devices: a whole 4x4x8 slice. The times are simulated.
256 devices in a mesh: dp: 16 (over z, core), proto: 16 (over x, y).
Axes of the slice: x: 4, y: 4, z: 8, core: 2. Of those that a mesh axis runs over, the one named last changes fastest.
Arguments:
- student_rows: bfloat16 [64, 256, 256], P('dp'), may hold values from -8 to 8
- teacher_rows: bfloat16 [64, 256, 256], P('dp'), may hold values from -8 to 8
- prototypes: bfloat16 [256, 131072], P(None, 'proto'), may hold values from -8 to 8
- center: float32 [131072], P('proto'), may hold values from -1.2 to 1.2
- mask_index: int32 [64, 128], P('dp'), may hold values from 0 to 255, as said below
- mask_count: int32 [64], P('dp'), may hold values from 0 to 128, as said below
- loss_scale: float32 [], replicated, may hold values from 1024 to 4096
Outputs:
- loss: float32 [], replicated
- student_grad: float32 [64, 256, 256], P('dp')
- proto_grad: float32 [131072, 256], P(('proto', 'dp'))
- patch_center: float32 [131072], P('proto')
Inputs may be any that keep to these rules, and one draw needn't show every extreme that they name: `mask_index`: for each image the first mask_count entries are distinct patch numbers; the later entries are patch numbers that are ignored. `mask_count`: the counts of all 64 images sum to 4096; some images have no masked patch.
All inputs are finite; a program needn't handle non-finite values.
Results may differ from a plain program's by a relative error of at most 0.022.
Values may be sent and summed in bfloat16 or wider, within the bound.
No kernel may reach another device: no remote copies, remote signals or barrier semaphores. Data moves between devices by JAX's collectives and lax.ppermute only.
A program may use at most 128 MiB of HBM per device.

v0:
```python
import jax
import jax.numpy as jnp
from jax import lax
from jax.sharding import PartitionSpec as P

teacher_temp = 0.04
student_temp = 0.1
norm_epsilon = 1e-06


def joined(value, axis, join):
    pieces = jax.tree.map(lambda part: lax.all_gather(part, axis), value)
    head = jax.tree.map(lambda part: part[0], pieces)
    tail = jax.tree.map(lambda part: part[1:], pieces)
    so_far, _ = lax.scan(lambda so_far, slab: (join(so_far, slab), None), head, tail)
    return so_far


def unit_rows(raw):
    values = raw.astype(jnp.float32)
    length = jnp.sqrt(jnp.sum(values * values, axis=1, keepdims=True) + norm_epsilon)
    return (values / length, length)


def merge_stats(first, second):
    t_top = jnp.maximum(first[0], second[0])
    t_left = jnp.exp(first[0] - t_top)
    t_right = jnp.exp(second[0] - t_top)
    s_top = jnp.maximum(first[3], second[3])
    s_left = jnp.exp(first[3] - s_top)
    s_right = jnp.exp(second[3] - s_top)
    return (
        t_top,
        first[1] * t_left + second[1] * t_right,
        first[2] * t_left + second[2] * t_right,
        s_top,
        first[4] * s_left + second[4] * s_right,
    )


def norm_backward(d_unit, s_unit, s_len):
    return (d_unit - s_unit * jnp.sum(s_unit * d_unit, axis=1, keepdims=True)) / s_len


def shards(student_rows, teacher_rows, prototypes, center, mask_index, mask_count, loss_scale):
    img_local, patches, width = student_rows.shape
    max_masked = mask_index.shape[1]
    data_size = lax.axis_size("dp")
    images = img_local * data_size
    padded_rows = img_local * max_masked
    total = images * max_masked // 2
    slots = jnp.arange(max_masked, dtype=jnp.int32)
    valid = slots[None, :] < mask_count[:, None]
    flat_valid = valid.reshape(-1)
    image_ids = jnp.arange(img_local, dtype=jnp.int32)[:, None]
    picked_s = student_rows[image_ids, mask_index].reshape(padded_rows, width)
    picked_t = teacher_rows[image_ids, mask_index].reshape(padded_rows, width)
    s_rows, t_rows = (picked_s, picked_t)
    count_f = jnp.maximum(mask_count, 1).astype(jnp.float32)
    weight = jnp.where(valid, 1.0 / (images * count_f[:, None]), 0.0).reshape(-1)
    live = flat_valid.astype(jnp.float32)
    s_unit, s_len = unit_rows(s_rows)
    t_unit, t_len = unit_rows(t_rows)
    s_half = s_unit.astype(jnp.bfloat16)
    t_half = t_unit.astype(jnp.bfloat16)
    s_logit = jnp.dot(s_half, prototypes, preferred_element_type=jnp.float32)
    t_logit = jnp.dot(t_half, prototypes, preferred_element_type=jnp.float32)
    col_sum = jnp.sum(t_logit * live[:, None], axis=0)
    t_arg = (t_logit - center[None, :]) / teacher_temp
    t_top = jnp.max(t_arg, axis=1)
    t_exp = jnp.exp(t_arg - t_top[:, None])
    s_arg = s_logit / student_temp
    s_top = jnp.max(s_arg, axis=1)
    s_exp = jnp.exp(s_arg - s_top[:, None])
    local_stats = (
        t_top,
        jnp.sum(t_exp, axis=1),
        jnp.sum(t_exp * s_arg, axis=1),
        s_top,
        jnp.sum(s_exp, axis=1),
    )
    t_all, t_total, cross, s_all, s_total = joined(local_stats, "proto", merge_stats)
    t_prob = t_exp * (jnp.exp(t_top - t_all) / t_total)[:, None]
    s_prob = s_exp * (jnp.exp(s_top - s_all) / s_total)[:, None]
    s_lse = s_all + jnp.log(s_total)
    ce = s_lse - cross / t_total
    loss_part = jnp.sum(weight * ce)
    col_total, loss = (
        lax.psum(col_sum.astype(jnp.bfloat16), "dp").astype(jnp.float32),
        lax.psum(loss_part.astype(jnp.bfloat16), "dp").astype(jnp.float32),
    )
    patch_center = col_total / total
    dlogit = (loss_scale * weight[:, None] * (s_prob - t_prob) / student_temp).astype(jnp.bfloat16)
    proto_grad = lax.psum_scatter(
        lax.dot_general(
            dlogit, s_half, (((0,), (0,)), ((), ())), preferred_element_type=jnp.float32
        ),
        "dp",
        scatter_dimension=0,
        tiled=True,
    )
    d_part = lax.dot_general(
        dlogit, prototypes, (((1,), (1,)), ((), ())), preferred_element_type=jnp.float32
    )
    d_unit = lax.psum(d_part, "proto")
    row_grads = norm_backward(d_unit, s_unit, s_len)
    rows_back = row_grads * live[:, None]
    student_grad = (
        jnp.zeros((img_local, patches, width), jnp.float32)
        .at[image_ids, mask_index]
        .add(rows_back.reshape(img_local, max_masked, width))
    )
    return (loss, student_grad, proto_grad, patch_center)


def solution(mesh):
    in_specs = (
        P("dp", None, None),
        P("dp", None, None),
        P(None, "proto"),
        P("proto"),
        P("dp", None),
        P("dp"),
        P(),
    )
    out_specs = (P(), P("dp", None, None), P(("proto", "dp"), None), P("proto"))
    return jax.shard_map(shards, mesh=mesh, in_specs=in_specs, out_specs=out_specs, check_vma=False)
```

profile of v0, /device:TPU:8, one launch (start us, length us, event | category | flops | bytes accessed | tf_op | source)
XLA Modules:
  0.0 319.8 jit_solution(8445233237288332)
XLA Ops:
  8.0 0.0 copy-start
  8.0 0.0 copy-start.6
  8.0 0.0 all-reduce.3.cloned.1.call-start
  8.1 0.7 select_bitcast_fusion
  8.8 0.3 copy-done
  9.1 3.2 gather_fusion.1
  12.2 0.1 fusion.5
  12.4 7.0 %gather_fusion = bf16[512,256]{1,0:T(8,128)(2,1)S(1)} fusion(bf16[4,256,256]{2,1,0:T(8,128)(2,1)} %param.10, s32[512]{0:T(512)S(1)} %get-tuple-element.108), kind=kCustom, calls=%fused_computation | custom fusion | bytes 528384 | tf_op jit(solution)/shard_map/gather | solution.py:57
  19.4 0.0 copy-start.3
  19.4 0.1 fusion.3
  19.6 0.9 convert_bitcast_fusion
  20.5 4.6 %multiply_reduce_fusion.2 = (f32[512]{0:T(512)S(1)}, f32[512,8192]{1,0:T(8,128)S(1)}) fusion(bf16[256,8192]{1,0:T(8,128)(2,1)} %param.11, f32[512]{0:T(512)S(1)} %add_sqrt_fusion, bf16[512,256]{1,0:T(8,128)(2,1)S(1)} %gather_fusion.1), kind=kOutput, calls=%fused_computation.21 | convolution fusion | flops 2156264960 | bytes 21237760 | tf_op jit(solution)/shard_map/dot_general | solution.py:66
  25.1 0.0 copy-done.6
  25.1 0.0 copy-done.3
  25.1 0.0 copy-start.1
  25.1 7.9 %fusion = (f32[512]{0:T(512)S(1)}, f32[512,8192]{1,0:T(8,128)}) fusion(f32[8192]{0:T(1024)S(1)} %copy-done.6, bf16[256,8192]{1,0:T(8,128)(2,1)S(1)} %copy-done.3, bf16[512,256]{1,0:T(8,128)(2,1)S(1)} %gather_fusion, f32[512]{0:T(512)S(1)} %add_sqrt_fusion.1), kind=kOutput, calls=%fused_computation.19 | convolution fusion | flops 2160459264 | bytes 21270528 | tf_op jit(solution)/shard_map/dot_general | solution.py:67
  33.0 0.0 copy-start.7
  33.0 16.1 %multiply_reduce_fusion.1 = (f32[512]{0:T(512)S(1)}, f32[512]{0:T(512)S(1)}, bf16[8192]{0:T(1024)(128)(2,1)S(1)}, f32[512]{0:T(512)S(1)}) fusion(f32[512,8192]{1,0:T(8,128)S(1)} %get-tuple-element.113, f32[512,8192]{1,0:T(8,128)} %get-tuple-element.111, f32[512]{0:T(512)S(1)} %get-tuple-element.110, f32[8192]{0:T(1024)S(1)} %copy-done.6, ...), kind=kLoop, calls=%fused_computation.16 | loop fusion | flops 46127616 | bytes 33615872 | tf_op jit(solution)/shard_map/reduce_sum | solution.py:78
  49.1 0.0 copy-done.1
  49.1 23.2 %all-gather.6 = f32[16,1,512]{2,1,0:T(1,128)S(1)} all-gather(f32[1,1,512]{2,1,0:T(1,128)S(1)} %bitcast.86), channel_id=3, replica_groups=mesh['dp'=16,'proto'=16] {'proto'}, dimensions={0}, use_global_device_ids=true | all-gather | bytes 34816 | tf_op jit(solution)/shard_map/all_gather | solution.py:12
  72.4 21.6 %all-gather.7 = f32[16,1,512]{2,1,0:T(1,128)S(1)} all-gather(f32[1,1,512]{2,1,0:T(1,128)S(1)} %bitcast.85), channel_id=4, replica_groups=mesh['dp'=16,'proto'=16] {'proto'}, dimensions={0}, use_global_device_ids=true | all-gather | bytes 34816 | tf_op jit(solution)/shard_map/all_gather | solution.py:12
  94.0 22.1 %all-gather.9 = f32[16,1,512]{2,1,0:T(1,128)S(1)} all-gather(f32[1,1,512]{2,1,0:T(1,128)S(1)} %bitcast.84), channel_id=6, replica_groups=mesh['dp'=16,'proto'=16] {'proto'}, dimensions={0}, use_global_device_ids=true | all-gather | bytes 34816 | tf_op jit(solution)/shard_map/all_gather | solution.py:12
  116.1 21.5 %all-gather.8 = f32[16,1,512]{2,1,0:T(1,128)S(1)} all-gather(f32[1,1,512]{2,1,0:T(1,128)S(1)} %bitcast.82), channel_id=5, replica_groups=mesh['dp'=16,'proto'=16] {'proto'}, dimensions={0}, use_global_device_ids=true | all-gather | bytes 34816 | tf_op jit(solution)/shard_map/all_gather | solution.py:12
  137.7 22.4 %all-gather.5 = f32[16,1,512]{2,1,0:T(1,128)S(1)} all-gather(f32[1,1,512]{2,1,0:T(1,128)S(1)} %bitcast.83), channel_id=2, replica_groups=mesh['dp'=16,'proto'=16] {'proto'}, dimensions={0}, use_global_device_ids=true | all-gather | bytes 34816 | tf_op jit(solution)/shard_map/all_gather | solution.py:12
  160.1 0.0 copy-done.7
  160.1 2.5 while.18
  163.3 0.7 exponential_divide_fusion.1
  164.0 0.0 copy-start.4
  164.0 14.6 %multiply_convert_fusion = bf16[512,8192]{1,0:T(8,128)(2,1)S(1)} fusion(f32[512,8192]{1,0:T(8,128)} %copy-done.1, f32[512,8192]{1,0:T(8,128)} %get-tuple-element.111, f32[512]{0:T(512)S(1)} %get-tuple-element.106, f32[512]{0:T(512)S(1)} %get-tuple-element.104, f32[512]{0:T(512)S(1)} %get-tuple-element.109, f32[512]{0:T(512)S(1)} %get-tuple-element.112, ...), kind=kLoop, calls=%fused_computation.14 | loop fusion | flops 46137344 | bytes 41986048 | tf_op jit(solution)/shard_map/convert_element_type | solution.py:93
  178.6 0.0 copy-start.5
  178.7 3.2 %copy-done.5 = bf16[512,8192]{1,0:T(8,128)(2,1)} copy-done((bf16[512,8192]{1,0:T(8,128)(2,1)}, bf16[512,8192]{1,0:T(8,128)(2,1)S(1)}, u32[]{:S(2)}) %copy-start.5) | copy-done | bytes 8388632
  181.9 0.0 copy-done.4
  181.9 3.2 fusion.19
  185.0 0.0 all-reduce.3.cloned.1.call-update
  185.0 0.0 reduce-scatter.2.cloned.1.call-start
  185.1 9.1 %fusion.9 = f32[8192,256]{1,0:T(8,128)} fusion(bf16[512,8192]{1,0:T(8,128)(2,1)} %copy-done.5, bf16[512,256]{1,0:T(8,128)(2,1)S(1)} %gather_fusion.1, f32[512]{0:T(512)S(1)} %add_sqrt_fusion), kind=kOutput, calls=%fused_computation.34 | convolution fusion | flops 2147876864 | bytes 17041408 | tf_op jit(solution)/shard_map/dot_general | solution.py:95
  194.2 0.0 reduce-scatter.2.cloned.1.call-update
  194.2 49.5 %all-reduce = (bf16[]{:T(256)}, bf16[8192]{0:T(1024)(128)(2,1)S(1)}) all-reduce(bf16[]{:T(256)} %get-tuple-element.105, bf16[8192]{0:T(1024)(128)(2,1)S(1)} %get-tuple-element.72), channel_id=1, replica_groups=mesh['dp'=16,'proto'=16] {'dp'}, use_global_device_ids=true, to_apply=%region_10.11 | all-reduce | flops 8193 | bytes 32772 | tf_op jit(solution)/shard_map/psum | solution.py:90
  244.4 0.6 convert_multiply_fusion.2
  245.0 36.3 %all-reduce.3.cloned.1.call-done = f32[512,256]{1,0:T(8,128)} async-done(((f32[512,256]{1,0:T(8,128)}), f32[512,256]{1,0:T(8,128)}) %all-reduce.3.cloned.1.call-update) | async-done | bytes 524304 | tf_op jit(solution)/shard_map/psum | solution.py:105
  281.3 1.3 multiply_reduce_fusion.3
  282.6 1.3 divide_multiply_fusion
  283.9 0.1 broadcast_in_dim.22
  284.0 26.2 %scatter_fusion = f32[4,256,256]{2,1,0:T(8,128)S(1)} fusion(f32[4,256,256]{2,1,0:T(8,128)S(1)} %broadcast_in_dim.22, s32[512]{0:T(512)S(1)} %get-tuple-element.107, f32[512,256]{1,0:T(8,128)S(1)} %divide_multiply_fusion), kind=kCustom, calls=%fused_computation.2 | custom fusion | flops 131072 | bytes 1576960 | tf_op jit(solution)/shard_map/scatter-add | solution.py:111
  310.2 0.0 copy-start.2
  310.2 0.0 reduce-scatter.2.cloned.1.call-done
  310.3 0.9 copy-done.2
  (138 shorter events, 1.6 us)
Async XLA Ops:
  8.0 1.1 copy-start
  8.0 17.1 %copy-start.6 = (f32[8192]{0:T(1024)S(1)}, f32[8192]{0:T(1024)}, u32[]{:S(2)}) copy-start(f32[8192]{0:T(1024)} %param.12) | copy-start | bytes 98308
  8.0 273.3 %all-reduce.3.cloned.1.call-start = ((), (), s32[]{:S(2)}) async-start(), calls=%async_computation.1 | async-start | bytes 1048576 | tf_op jit(solution)/shard_map/psum | solution.py:105
  19.4 5.7 %copy-start.3 = (bf16[256,8192]{1,0:T(8,128)(2,1)S(1)}, bf16[256,8192]{1,0:T(8,128)(2,1)}, u32[]{:S(2)}) copy-start(bf16[256,8192]{1,0:T(8,128)(2,1)} %param.11) | copy-start | bytes 12582916
  25.1 24.0 %copy-start.1 = (f32[512,8192]{1,0:T(8,128)}, f32[512,8192]{1,0:T(8,128)S(1)}, u32[]{:S(2)}) copy-start(f32[512,8192]{1,0:T(8,128)S(1)} %get-tuple-element.113) | copy-start | bytes 50331652
  33.0 127.1 %copy-start.7 = (s32[4]{0:T(128)S(1)}, s32[4]{0:T(128)}, u32[]{:S(2)}) copy-start(s32[4]{0:T(128)} %param.14) | copy-start | bytes 52
  164.0 17.9 %copy-start.4 = (bf16[256,8192]{1,0:T(8,128)(2,1)S(1)}, bf16[256,8192]{1,0:T(8,128)(2,1)}, u32[]{:S(2)}) copy-start(bf16[256,8192]{1,0:T(8,128)(2,1)} %param.11) | copy-start | bytes 12582916
  178.6 3.2 %copy-start.5 = (bf16[512,8192]{1,0:T(8,128)(2,1)}, bf16[512,8192]{1,0:T(8,128)(2,1)S(1)}, u32[]{:S(2)}) copy-start(bf16[512,8192]{1,0:T(8,128)(2,1)S(1)} %multiply_convert_fusion) | copy-start | bytes 25165828
  185.0 125.2 %reduce-scatter.2.cloned.1.call-start = ((), (), s32[]{:S(2)}) async-start(), calls=%async_computation.2 | async-start | bytes 8912896 | tf_op jit(solution)/shard_map/reduce_scatter | solution.py:94
  310.2 1.0 copy-start.2
Sparse Core Ops, SparseCore 0:
  185.2 96.1 all-reduce.2
Sparse Core Ops, SparseCore 1:
  194.3 72.1 reduce-scatter.1
where the time goes:
time: 320 us
  blocking collectives  160 us (50%)
  other arithmetic  63.4 us (20%)
  waiting for transfers between devices  36.3 us (11%)
  matrix products  24.7 us (8%)
  between operations  18.2 us (6%)
  local copies, waits for them, and re-layouts  15.7 us (5%)
    all_gather x5, blocking collectives, joined(): pieces = jax.tree.map(lambda part: lax.all_gather(part, axis), value)  111 us
    psum x1, blocking collectives, shards(): lax.psum(loss_part.astype(jnp.bfloat16), 'dp').astype(jnp.float32)  49.5 us
    psum x1, waiting for transfers between devices, shards(): d_unit = lax.psum(d_part, 'proto')  36.3 us
    scatter-add x1, other arithmetic, shards(): student_grad = jnp.zeros((img_local, patches, width), jnp.float32).at[ima...  26.2 us
    reduce_sum x1, other arithmetic, shards(): jnp.sum(t_exp * s_arg, axis=1)  16.1 us
    convert_element_type x1, other arithmetic, shards(): (loss_scale * weight[:, None] * (s_prob - t_prob) / student_temp).astype(...  14.6 us
    dot_general x1, matrix products, shards(): lax.dot_general(dlogit, s_half, (((0,), (0,)), ((), ())), preferred_eleme...  9.09 us
    dot_general x1, matrix products, shards(): t_logit = jnp.dot(t_half, prototypes, preferred_element_type=jnp.float32)  7.86 us
  transfers between devices with their start and end apart: 2, of which 1 were waited for; matrix products, arithmetic and copies ran while one was open for 12% of the time, Pallas kernels for 0%

commit v1 on v0

v1 whole, which is shorter than its diff:
```python
import functools
import math

import jax
import jax.numpy as jnp
from jax import lax
from jax.experimental import pallas as pl
from jax.experimental.pallas import tpu as pltpu
from jax.sharding import Mesh, PartitionSpec as P

bf16 = jnp.bfloat16
f32 = jnp.float32
log2e = math.log2(math.e)
ln2 = math.log(2.0)
t_scale = log2e / 0.04
s_scale = log2e / 0.1
inverse_temp = 10.0
norm_epsilon = 1e-06
low = -1e30

Z, CORES, X, Y = 8, 2, 4, 4
D = 256
SLOTS = 128
IMAGES = 64
TOTAL = 4096
LOCAL = 4
ROWS = LOCAL * SLOTS
BOTH = 2 * ROWS
CHUNK = 512
TILE = 256

NT = (((1,), (1,)), ((), ()))
TN = (((0,), (0,)), ((), ()))


def dot(a, b, dims=(((1,), (0,)), ((), ()))):
    return lax.dot_general(a, b, dims, preferred_element_type=f32)


def params():
    return pltpu.CompilerParams(vmem_limit_bytes=48 * 1024 * 1024)


def cost(flops, nbytes, trans=0):
    return pl.CostEstimate(flops=flops, bytes_accessed=nbytes, transcendentals=trans)


def picks(index_ref, count, i):
    patch = lax.broadcasted_iota(jnp.int32, (D, SLOTS), 0)
    slot = lax.broadcasted_iota(jnp.int32, (D, SLOTS), 1)
    hit = (patch == index_ref[i : i + 1, :]) & (slot < count)
    return jnp.where(hit, 1.0, 0.0).astype(bf16)


def unit_rows(values):
    length = jnp.sqrt(jnp.sum(values * values, axis=1, keepdims=True) + norm_epsilon)
    return values / length, length


def prep_kernel(count_ref, index_ref, s_ref, t_ref, out_ref):
    for i in range(LOCAL):
        pick = picks(index_ref, count_ref[i], i)
        for which, ref in enumerate((s_ref, t_ref)):
            unit, _ = unit_rows(dot(pick, ref[i], TN))
            out_ref[which, i * SLOTS : (i + 1) * SLOTS, :] = unit.astype(bf16)


def prep(count, index, student, teacher):
    smem = pl.BlockSpec(memory_space=pltpu.SMEM)
    vmem = pl.BlockSpec(memory_space=pltpu.VMEM)
    return pl.pallas_call(
        prep_kernel,
        out_shape=jax.ShapeDtypeStruct((2, ROWS, D), bf16),
        in_specs=[smem, vmem, vmem, vmem],
        out_specs=vmem,
        compiler_params=params(),
        cost_estimate=cost(2 * 2 * ROWS * D * D, 1 << 21),
    )(count, index, student, teacher)


def turn_kernel(ids_ref, p_ref, c_ref, pt_ref, cb_ref):
    pt_ref[0] = p_ref[...].T
    cb_ref[0] = jnp.broadcast_to(c_ref[0] * -t_scale, (128, CHUNK)).T


def turn(ids, prototypes, center):
    grid = pltpu.PrefetchScalarGridSpec(
        num_scalar_prefetch=1,
        grid=(Z,),
        in_specs=[
            pl.BlockSpec((D, CHUNK), lambda i, ids: (0, 2 * i + ids[1])),
            pl.BlockSpec((1, 1, CHUNK), lambda i, ids: (2 * i + ids[1], 0, 0)),
        ],
        out_specs=[
            pl.BlockSpec((1, CHUNK, D), lambda i, ids: (i, 0, 0)),
            pl.BlockSpec((1, CHUNK, 128), lambda i, ids: (i, 0, 0)),
        ],
    )
    return pl.pallas_call(
        turn_kernel,
        grid_spec=grid,
        out_shape=[
            jax.ShapeDtypeStruct((Z, CHUNK, D), bf16),
            jax.ShapeDtypeStruct((Z, CHUNK, 128), f32),
        ],
        compiler_params=params(),
        cost_estimate=cost(0, 6 << 20),
    )(ids, prototypes, center.reshape(2 * Z, 1, CHUNK))


def wide(block, times):
    return jnp.concatenate([block] * times, axis=1)


def stats_kernel(count_ref, pt_ref, cb_ref, mine_ref, other_ref, out_ref, sum_ref, acc):
    step = pl.program_id(0)

    @pl.when(step == 0)
    def _():
        acc[...] = jnp.zeros(acc.shape, f32)
        acc[0] = jnp.full((8, BOTH), low, f32)
        acc[3] = jnp.full((8, BOTH), low, f32)

    protos = pt_ref[0]
    shift = wide(cb_ref[0], TILE // 128)
    for half, ref in enumerate((mine_ref, other_ref)):
        for j in range(ROWS // TILE):
            rows = slice(j * TILE, (j + 1) * TILE)
            at = slice(half * ROWS + j * TILE, half * ROWS + (j + 1) * TILE)
            t_arg = (dot(protos, ref[1, rows, :], NT) * t_scale + shift).reshape(CHUNK // 8, 8, TILE)
            s_arg = (dot(protos, ref[0, rows, :], NT) * s_scale).reshape(CHUNK // 8, 8, TILE)
            t_old, s_old = acc[0, :, at], acc[3, :, at]
            t_top = jnp.maximum(t_old, jnp.max(t_arg, axis=0))
            s_top = jnp.maximum(s_old, jnp.max(s_arg, axis=0))
            t_exp = jnp.exp2(t_arg - t_top[None])
            s_exp = jnp.exp2(s_arg - s_top[None])
            t_keep = jnp.exp2(t_old - t_top)
            s_keep = jnp.exp2(s_old - s_top)
            acc[0, :, at] = t_top
            acc[1, :, at] = acc[1, :, at] * t_keep + jnp.sum(t_exp, axis=0)
            acc[2, :, at] = acc[2, :, at] * t_keep + jnp.sum(t_exp * s_arg, axis=0)
            acc[3, :, at] = s_top
            acc[4, :, at] = acc[4, :, at] * s_keep + jnp.sum(s_exp, axis=0)

    @pl.when(step == Z - 1)
    def _():
        t_top = jnp.max(acc[0], axis=0, keepdims=True)
        s_top = jnp.max(acc[3], axis=0, keepdims=True)
        t_keep = jnp.exp2(acc[0] - t_top)
        s_keep = jnp.exp2(acc[3] - s_top)
        out_ref[0:1, :] = t_top
        out_ref[1:2, :] = jnp.sum(acc[1] * t_keep, axis=0, keepdims=True)
        out_ref[2:3, :] = jnp.sum(acc[2] * t_keep, axis=0, keepdims=True)
        out_ref[3:4, :] = s_top
        out_ref[4:5, :] = jnp.sum(acc[4] * s_keep, axis=0, keepdims=True)
        out_ref[5:8, :] = jnp.zeros((3, BOTH), f32)
        slot = lax.broadcasted_iota(jnp.int32, (1, SLOTS), 1)
        for i in range(LOCAL):
            count = jnp.full((1, SLOTS), count_ref[i], jnp.int32)
            weight = 1.0 / (IMAGES * jnp.maximum(count, 1).astype(f32))
            out_ref[5:6, i * SLOTS : (i + 1) * SLOTS] = jnp.where(slot < count, weight, 0.0)
        first = jnp.sum(mine_ref[1].astype(f32), axis=0, keepdims=True)
        second = jnp.sum(other_ref[1].astype(f32), axis=0, keepdims=True)
        sum_ref[...] = jnp.broadcast_to(first + second, (8, D))


def local_stats(count, turned, shifts, mine, other):
    whole = pl.BlockSpec((2, ROWS, D), lambda i, n: (0, 0, 0))
    grid = pltpu.PrefetchScalarGridSpec(
        num_scalar_prefetch=1,
        grid=(Z,),
        in_specs=[
            pl.BlockSpec((1, CHUNK, D), lambda i, n: (i, 0, 0)),
            pl.BlockSpec((1, CHUNK, 128), lambda i, n: (i, 0, 0)),
            whole,
            whole,
        ],
        out_specs=[
            pl.BlockSpec((8, BOTH), lambda i, n: (0, 0)),
            pl.BlockSpec((8, D), lambda i, n: (0, 0)),
        ],
        scratch_shapes=[pltpu.VMEM((5, 8, BOTH), f32)],
    )
    return pl.pallas_call(
        stats_kernel,
        grid_spec=grid,
        out_shape=[jax.ShapeDtypeStruct((8, BOTH), f32), jax.ShapeDtypeStruct((8, D), f32)],
        compiler_params=params(),
        cost_estimate=cost(4 * BOTH * Z * CHUNK * D, 6 << 20, 2 * BOTH * Z * CHUNK),
    )(count, turned, shifts, mine, other)


def tree(parts):
    while len(parts) > 1:
        parts = [parts[i] + parts[i + 1] for i in range(0, len(parts), 2)]
    return parts[0]


def merged(parts):
    t_top = functools.reduce(jnp.maximum, [p[0:1] for p in parts])
    s_top = functools.reduce(jnp.maximum, [p[3:4] for p in parts])
    t_keep = [jnp.exp2(p[0:1] - t_top) for p in parts]
    s_keep = [jnp.exp2(p[3:4] - s_top) for p in parts]
    t_sum = tree([p[1:2] * k for p, k in zip(parts, t_keep)])
    cross = tree([p[2:3] * k for p, k in zip(parts, t_keep)])
    s_sum = tree([p[4:5] * k for p, k in zip(parts, s_keep)])
    return t_top, t_sum, cross, s_top, s_sum


def core_merge_kernel(mine_ref, got_ref, out_ref):
    mine = mine_ref[...]
    got = jnp.concatenate([got_ref[:, ROWS:], got_ref[:, :ROWS]], axis=1)
    for i, row in enumerate(merged([mine, got])):
        out_ref[i : i + 1, :] = row
    out_ref[5:6, :] = mine[5:6] + got[5:6]
    out_ref[6:8, :] = jnp.zeros((2, BOTH), f32)


def merge_kernel(*refs):
    out_ref = refs[-1]
    parts = [ref[...] for ref in refs[:-1]]
    for i, row in enumerate(merged(parts)):
        out_ref[i : i + 1, :] = row
    out_ref[5:8, :] = parts[0][5:8]


def last_merge_kernel(scale_ref, a, b, c, d, sum_ref, coef_ref, misc_ref):
    parts = [ref[...] for ref in (a, b, c, d)]
    t_top, t_sum, cross, s_top, s_sum = merged(parts)
    weight = parts[0][5:6]
    live = weight > 0.0
    s_lse = s_top + jnp.log2(s_sum)
    ce = (s_lse - cross / t_sum) * ln2
    factor = jnp.log2(jnp.where(live, weight * (scale_ref[0] * inverse_temp), 1.0))
    coef_ref[0:1, :] = jnp.where(live, factor - s_lse, low)
    coef_ref[1:2, :] = jnp.where(live, factor - t_top - jnp.log2(t_sum), low)
    coef_ref[2:8, :] = jnp.zeros((6, BOTH), f32)
    part = jnp.where(live, weight * ce, 0.0)
    first = jnp.sum(part[:, :ROWS], axis=1, keepdims=True)
    second = jnp.sum(part[:, ROWS:], axis=1, keepdims=True)
    misc_ref[0:1, :] = sum_ref[0:1, :]
    misc_ref[1:8, :] = jnp.broadcast_to(first + second, (7, D))


def small_call(kernel, out_shape, *args, smem=()):
    specs = [
        pl.BlockSpec(memory_space=pltpu.SMEM if i in smem else pltpu.VMEM) for i in range(len(args))
    ]
    vmem = pl.BlockSpec(memory_space=pltpu.VMEM)
    return pl.pallas_call(
        kernel,
        out_shape=out_shape,
        in_specs=specs,
        out_specs=jax.tree.map(lambda _: vmem, out_shape),
        compiler_params=params(),
        cost_estimate=cost(1 << 20, 1 << 18),
    )(*args)


def swapped(axis, size, bit):
    return [(i, i ^ bit) for i in range(size)]


def swap(value, axis, size, bit):
    return lax.ppermute(value, axis, swapped(axis, size, bit))


def grad_kernel(n, split, ids_ref, order_ref, pt_ref, cb_ref, p_ref, mine_ref, other_ref, coef_ref, *refs):
    out_refs, du_ref = refs[:-1], refs[-1]
    step = pl.program_id(0)
    protos = pt_ref[0]
    shift = wide(cb_ref[0], TILE // 128)
    wide_p = p_ref[...]
    total = None
    for half, ref in enumerate((mine_ref, other_ref)):
        for j in range(ROWS // TILE):
            rows = slice(j * TILE, (j + 1) * TILE)
            at = slice(half * ROWS + j * TILE, half * ROWS + (j + 1) * TILE)
            s_rows = ref[0, rows, :]
            t_arg = dot(protos, ref[1, rows, :], NT) * t_scale + shift + coef_ref[1:2, at]
            s_arg = dot(protos, s_rows, NT) * s_scale + coef_ref[0:1, at]
            dlogit = (jnp.exp2(s_arg) - jnp.exp2(t_arg)).astype(bf16)
            part = dot(dlogit, s_rows)
            total = part if total is None else total + part
            du = dot(wide_p, dlogit)

            @pl.when(step == 0)
            def _(at=at, du=du):
                du_ref[:, at] = du

            @pl.when(step > 0)
            def _(at=at, du=du):
                du_ref[:, at] += du

    if split:
        out_refs[0][...] = total[: CHUNK // 2].astype(bf16)
        out_refs[1][...] = total[CHUNK // 2 :].astype(bf16)
    else:
        out_refs[0][0] = total


def grads(ids, offsets, split, turned, shifts, prototypes, mine, other, coef):
    n = len(offsets)
    order = lax.rem(ids[0] + jnp.array([d % Z for d in offsets], jnp.int32), Z)
    whole = pl.BlockSpec((2, ROWS, D), lambda i, ids, order: (0, 0, 0))
    if split:
        outs = [jax.ShapeDtypeStruct((CHUNK // 2, D), bf16)] * 2
        specs = [pl.BlockSpec((CHUNK // 2, D), lambda i, ids, order: (0, 0))] * 2
    else:
        outs = [jax.ShapeDtypeStruct((n, CHUNK, D), f32)]
        specs = [pl.BlockSpec((1, CHUNK, D), lambda i, ids, order: (i, 0, 0))]
    grid = pltpu.PrefetchScalarGridSpec(
        num_scalar_prefetch=2,
        grid=(n,),
        in_specs=[
            pl.BlockSpec((1, CHUNK, D), lambda i, ids, order: (order[i], 0, 0)),
            pl.BlockSpec((1, CHUNK, 128), lambda i, ids, order: (order[i], 0, 0)),
            pl.BlockSpec((D, CHUNK), lambda i, ids, order: (0, 2 * order[i] + ids[1])),
            whole,
            whole,
            pl.BlockSpec((8, BOTH), lambda i, ids, order: (0, 0)),
        ],
        out_specs=specs + [pl.BlockSpec((D, BOTH), lambda i, ids, order: (0, 0))],
    )
    return pl.pallas_call(
        functools.partial(grad_kernel, n, split),
        grid_spec=grid,
        out_shape=outs + [jax.ShapeDtypeStruct((D, BOTH), f32)],
        compiler_params=params(),
        cost_estimate=cost(8 * BOTH * n * CHUNK * D, 3 << 20, 2 * BOTH * n * CHUNK),
    )(ids, order, turned, shifts, prototypes, mine, other, coef)


def du_send_kernel(a, b, c, out_ref):
    out_ref[...] = (a[:, ROWS:] + b[:, ROWS:] + c[:, ROWS:]).astype(bf16)


def du_first_kernel(ids_ref, a, b, c, got_ref, *refs):
    outs, total = refs[:4], refs[4]
    total[...] = a[:, :ROWS] + b[:, :ROWS] + c[:, :ROWS] + got_ref[...].astype(f32)
    y = ids_ref[3]
    for k in range(Y):
        start = pl.multiple_of(jnp.bitwise_xor(y, k) * (D // Y), D // Y)
        outs[k][...] = total[pl.ds(start, D // Y), :].astype(bf16)


def du_second_kernel(ids_ref, a, b, c, d, *refs):
    outs, total = refs[:4], refs[4]
    total[...] = a[...].astype(f32) + b[...].astype(f32) + c[...].astype(f32) + d[...].astype(f32)
    x = ids_ref[2]
    part = D // (Y * X)
    for k in range(X):
        start = pl.multiple_of(jnp.bitwise_xor(x, k) * part, part)
        outs[k][...] = total[pl.ds(start, part), :].astype(bf16)


def du_sum_kernel(a, b, c, d, out_ref):
    out_ref[...] = (a[...].astype(f32) + b[...].astype(f32) + c[...].astype(f32) + d[...].astype(f32)).astype(bf16)


def du_join_kernel(ids_ref, a, b, c, d, out_ref, held):
    part = D // (Y * X)
    x = ids_ref[2]
    for k, ref in enumerate((a, b, c, d)):
        start = pl.multiple_of(jnp.bitwise_xor(x, k) * part, part)
        held[pl.ds(start, part), :] = ref[...].astype(f32)
    out_ref[...] = held[...].astype(bf16)


def final_kernel(ids_ref, count_ref, index_ref, s_ref, a, b, c, d, out_ref, held):
    y = ids_ref[3]
    for k, ref in enumerate((a, b, c, d)):
        start = pl.multiple_of(jnp.bitwise_xor(y, k) * (D // Y), D // Y)
        held[pl.ds(start, D // Y), :] = ref[...].astype(f32)
    for i in range(LOCAL):
        pick = picks(index_ref, count_ref[i], i)
        unit, length = unit_rows(dot(pick, s_ref[i], TN))
        d_unit = held[:, i * SLOTS : (i + 1) * SLOTS].T
        row = (d_unit - unit * jnp.sum(unit * d_unit, axis=1, keepdims=True)) / length
        top = row.astype(bf16)
        rest = (row - top.astype(f32)).astype(bf16)
        out_ref[i] = dot(pick, top) + dot(pick, rest)


def scratch_call(kernel, out_shape, scratch, *args, smem=()):
    specs = [
        pl.BlockSpec(memory_space=pltpu.SMEM if i in smem else pltpu.VMEM) for i in range(len(args))
    ]
    vmem = pl.BlockSpec(memory_space=pltpu.VMEM)
    return pl.pallas_call(
        kernel,
        out_shape=out_shape,
        in_specs=specs,
        out_specs=jax.tree.map(lambda _: vmem, out_shape),
        scratch_shapes=scratch,
        compiler_params=params(),
        cost_estimate=cost(1 << 20, 1 << 20),
    )(*args)


def center_kernel(misc_ref, p_ref, out_ref):
    total = jnp.broadcast_to(misc_ref[0:1, :], (8, D))
    top = total.astype(bf16)
    rest = total - top.astype(f32)
    middle = rest.astype(bf16)
    last = (rest - middle.astype(f32)).astype(bf16)
    p = p_ref[...]
    out_ref[...] = (dot(top, p) + dot(middle, p) + dot(last, p)) * (1.0 / TOTAL)


def centers(misc, prototypes):
    width = prototypes.shape[1]
    block = 2048
    out = pl.pallas_call(
        center_kernel,
        grid=(width // block,),
        in_specs=[
            pl.BlockSpec((8, D), lambda i: (0, 0)),
            pl.BlockSpec((D, block), lambda i: (0, i)),
        ],
        out_specs=pl.BlockSpec((8, block), lambda i: (0, i)),
        out_shape=jax.ShapeDtypeStruct((8, width), f32),
        compiler_params=params(),
        cost_estimate=cost(6 * 8 * D * width, 5 << 20),
    )(misc, prototypes)
    return out[0]


def shards(student_rows, teacher_rows, prototypes, center, mask_index, mask_count, loss_scale):
    z, core, x, y = (lax.axis_index(a) for a in ("z", "core", "x", "y"))
    ids = jnp.stack([z, core, x, y]).astype(jnp.int32)
    down = [(i, (i - 1) % Z) for i in range(Z)]
    up = [(i, (i + 1) % Z) for i in range(Z)]

    mine = prep(mask_count, mask_index, student_rows, teacher_rows)
    other = swap(mine, "core", CORES, 1)
    turned, shifts = turn(ids, prototypes, center)
    stats, row_sum = local_stats(mask_count, turned, shifts, mine, other)

    shape = jax.ShapeDtypeStruct((8, BOTH), f32)
    stats = small_call(core_merge_kernel, shape, stats, swap(stats, "core", CORES, 1))
    stats = small_call(merge_kernel, shape, stats, *[swap(stats, "y", Y, k) for k in (1, 2, 3)])
    coef, misc = small_call(
        last_merge_kernel,
        [shape, jax.ShapeDtypeStruct((8, D), f32)],
        loss_scale.reshape(1),
        stats,
        *[swap(stats, "x", X, k) for k in (1, 2, 3)],
        row_sum,
        smem=(0,),
    )

    common = (turned, shifts, prototypes, mine, other, coef)
    half_a, half_b, du_a = grads(ids, [4], True, *common)
    from_up = lax.ppermute(half_a, "z", down)
    from_down = lax.ppermute(half_b, "z", up)
    far, du_b = grads(ids, [-3, 3], False, *common)
    half = CHUNK // 2
    send_down = jnp.concatenate([far[0, :half] + from_up.astype(f32), far[0, half:]]).astype(bf16)
    send_up = jnp.concatenate([far[1, :half], far[1, half:] + from_down.astype(f32)]).astype(bf16)
    from_up = lax.ppermute(send_down, "z", down)
    from_down = lax.ppermute(send_up, "z", up)
    near, du_c = grads(ids, [-2, 2, -1, 1, 0], False, *common)
    from_up = lax.ppermute((near[0] + from_up.astype(f32)).astype(bf16), "z", down)
    from_down = lax.ppermute((near[1] + from_down.astype(f32)).astype(bf16), "z", up)
    from_up = lax.ppermute((near[2] + from_up.astype(f32)).astype(bf16), "z", down)
    from_down = lax.ppermute((near[3] + from_down.astype(f32)).astype(bf16), "z", up)
    proto_grad = near[4] + from_up.astype(f32) + from_down.astype(f32)

    for bit in (1, 2, 4):
        misc = misc + swap(misc, "z", Z, bit)
    loss = misc[1, 0]
    patch_center = centers(misc, prototypes)

    send = small_call(du_send_kernel, jax.ShapeDtypeStruct((D, ROWS), bf16), du_a, du_b, du_c)
    got = swap(send, "core", CORES, 1)
    part = D // Y
    pieces = scratch_call(
        du_first_kernel,
        [jax.ShapeDtypeStruct((part, ROWS), bf16)] * Y,
        [pltpu.VMEM((D, ROWS), f32)],
        ids, du_a, du_b, du_c, got,
        smem=(0,),
    )
    got = [swap(pieces[k], "y", Y, k) for k in (1, 2, 3)]
    pieces = scratch_call(
        du_second_kernel,
        [jax.ShapeDtypeStruct((part // X, ROWS), bf16)] * X,
        [pltpu.VMEM((part, ROWS), f32)],
        ids, pieces[0], *got,
        smem=(0,),
    )
    got = [swap(pieces[k], "x", X, k) for k in (1, 2, 3)]
    own = small_call(du_sum_kernel, jax.ShapeDtypeStruct((part // X, ROWS), bf16), pieces[0], *got)
    got = [swap(own, "x", X, k) for k in (1, 2, 3)]
    own = scratch_call(
        du_join_kernel,
        jax.ShapeDtypeStruct((part, ROWS), bf16),
        [pltpu.VMEM((part, ROWS), f32)],
        ids, own, *got,
        smem=(0,),
    )
    got = [swap(own, "y", Y, k) for k in (1, 2, 3)]
    student_grad = scratch_call(
        final_kernel,
        jax.ShapeDtypeStruct(student_rows.shape, f32),
        [pltpu.VMEM((D, ROWS), f32)],
        ids, mask_count, mask_index, student_rows, own, *got,
        smem=(0, 1),
    )
    return (loss, student_grad, proto_grad, patch_center)


def solution(mesh):
    fine = Mesh(mesh.devices.reshape(Z, CORES, X, Y), ("z", "core", "x", "y"))
    dp, proto = ("z", "core"), ("x", "y")
    in_specs = (
        P(dp, None, None),
        P(dp, None, None),
        P(None, proto),
        P(proto),
        P(dp, None),
        P(dp),
        P(),
    )
    out_specs = (P(), P(dp, None, None), P(proto + dp, None), P(proto))
    return jax.shard_map(shards, mesh=fine, in_specs=in_specs, out_specs=out_specs, check_vma=False)
```

time: 320 us -> 138 us (0.43)
  blocking collectives: 160 us -> 0 us
  other arithmetic: 63.4 us -> 5.71 us
  Pallas kernels: 0 us -> 50.5 us
  starting transfers between devices: 0.08 us -> 49.5 us
  matrix products: 24.7 us -> 0 us
  between operations: 18.2 us -> 1.61 us
  waiting for transfers between devices: 36.3 us -> 22.2 us
  local copies, waits for them, and re-layouts: 15.7 us -> 5.4 us
    all_gather x5 -> x0, blocking collectives: 111 us -> none  [joined(): pieces = jax.tree.map(lambda part: lax.all_gather(part, axis), value)]
    pallas_call x0 -> x16, Pallas kernels: none -> 50.5 us  [the longest x3 23.4 us: grads(): pl.pallas_call(functools.partial(grad_kernel, n, split), grid_spec=grid,...]
    psum x1 -> x0, blocking collectives: 49.5 us -> none  [shards(): lax.psum(loss_part.astype(jnp.bfloat16), 'dp').astype(jnp.float32)]
    ppermute x0 -> x32, starting transfers between devices: none -> 49.5 us  [the longest x24 32.7 us: swap(): return lax.ppermute(value, axis, swapped(axis, size, bit))]
    psum x1 -> x0, waiting for transfers between devices: 36.3 us -> none  [shards(): d_unit = lax.psum(d_part, 'proto')]
    scatter-add x1 -> x0, other arithmetic: 26.2 us -> none  [shards(): student_grad = jnp.zeros((img_local, patches, width), jnp.float32).at[ima...]
    dot_general x4 -> x0, matrix products: 24.7 us -> none  [the longest x1 9.09 us: shards(): lax.dot_general(dlogit, s_half, (((0,), (0,)), ((), ())), preferred_eleme...]
    ppermute x0 -> x32, waiting for transfers between devices: none -> 22.2 us  [the longest x24 14.3 us: swap(): return lax.ppermute(value, axis, swapped(axis, size, bit))]
  transfers between devices with their start and end apart: 2 -> 32, of which waited for: 1 -> 13; matrix products, arithmetic and copies ran while one was open for 12% -> 3% of each run, Pallas kernels for 0% -> 24%
where the time goes in v1:
time: 138 us; the launch traced here: 135 us
  Pallas kernels  50.5 us (37%)
  starting transfers between devices  49.5 us (36%)
  waiting for transfers between devices  22.2 us (16%)
  other arithmetic  5.71 us (4%)
  local copies, waits for them, and re-layouts  5.4 us (4%)
  between operations  1.61 us (1%)
    ppermute x24, starting transfers between devices, swap(): return lax.ppermute(value, axis, swapped(axis, size, bit))  32.7 us
    pallas_call x3, Pallas kernels, grads(): pl.pallas_call(functools.partial(grad_kernel, n, split), grid_spec=grid,...  23.4 us
    ppermute x24, waiting for transfers between devices, swap(): return lax.ppermute(value, axis, swapped(axis, size, bit))  14.3 us
    pallas_call x1, Pallas kernels, local_stats(): pl.pallas_call(stats_kernel, grid_spec=grid, out_shape=[jax.ShapeDtypeStr...  13.2 us
    ppermute x1, starting transfers between devices, shards(): from_up = lax.ppermute(half_a, 'z', down)  5.93 us
    pallas_call x1, Pallas kernels, turn(): pl.pallas_call(turn_kernel, grid_spec=grid, out_shape=[jax.ShapeDtypeStru...  5.48 us
    pallas_call x4, Pallas kernels, scratch_call(): pl.pallas_call(kernel, out_shape=out_shape, in_specs=specs, out_specs=jax...  4.76 us
    unnamed x24, local copies, waits for them, and re-layouts  4.21 us
  transfers between devices with their start and end apart: 32, of which 13 were waited for; matrix products, arithmetic and copies ran while one was open for 3% of the time, Pallas kernels for 24%

profile of v1, /device:TPU:8, one launch (start us, length us, event | category | flops | bytes accessed | tf_op | source)
XLA Modules:
  0.0 134.9 jit_solution(6884614813074810468)
XLA Ops:
  0.6 1.0 copy-done.2
  1.7 1.0 copy-done.4
  2.7 0.7 copy-done.6
  3.4 0.7 copy-done.8
  4.1 1.1 shard_map.130.mine_ref
  5.1 0.1 collective-permute-start
  5.3 0.8 copy-done.5
  6.1 5.5 %shard_map.129 = (bf16[8,512,256]{2,1,0:T(8,128)(2,1)S(1)}, f32[8,512,128]{2,1,0:T(8,128)S(1)}) custom-call(s32[4]{0:T(128)S(1)} %pad_add_fusion.ids_ref, bf16[256,8192]{1,0:T(8,128)(2,1)} %p_ref.9, f32[16,1,512]{2,1,0:T(1,128)S(1)} %bitcast.41), custom_call_target="tpu_custom_call" | custom-call | bytes 6291456 | tf_op jit(solution)/shard_map/pallas_call | solution.py:99
  11.6 13.2 %shard_map.131 = (f32[8,1024]{1,0:T(8,128)S(1)}, f32[8,256]{1,0:T(8,128)S(1)}) custom-call(s32[4]{0:T(128)S(1)} %copy-done.9, bf16[8,512,256]{2,1,0:T(8,128)(2,1)S(1)} %get-tuple-element.25.pt_ref, f32[8,512,128]{2,1,0:T(8,128)S(1)} %get-tuple-element.26.cb_ref, bf16[2,512,256]{2,1,0:T(8,128)(2,1)S(1)} %shard_map.130.mine_ref, ...), custom_call_target="tpu_custom_call" | custom-call | flops 4294967296 | bytes 6291456 | tf_op jit(solution)/shard_map/pallas_call | solution.py:184
  24.8 0.6 collective-permute-start.1
  25.4 0.9 collective-permute-done.1.got_ref
  26.3 2.3 %collective-permute-start.2 = (f32[8,1024]{1,0:T(8,128)S(1)}, f32[8,1024]{1,0:T(8,128)S(1)}, u32[]{:S(2)}, u32[]{:S(2)}) collective-permute-start(f32[8,1024]{1,0:T(8,128)S(1)} %shard_map.132.refs_0_), channel_id=1, source_target_pairs={{0,1},{1,0},{2,3},{3,2},{4,5},{5,4},{6,7},{7,6},{8,9},{9,8},{10,11... | collective-permute-start | bytes 98312 | tf_op jit(solution)/shard_map/ppermute | solution.py:265
  28.5 0.8 collective-permute-start.3
  29.4 0.7 collective-permute-start.4
  30.1 0.3 collective-permute-done.2.refs_1_
  30.4 3.5 %collective-permute-done.3.refs_2_ = f32[8,1024]{1,0:T(8,128)S(1)} collective-permute-done((f32[8,1024]{1,0:T(8,128)S(1)}, f32[8,1024]{1,0:T(8,128)S(1)}, u32[]{:S(2)}, u32[]{:S(2)}) %collective-permute-start.3) | collective-permute-done | bytes 32800 | tf_op jit(solution)/shard_map/ppermute | solution.py:265
  34.0 0.9 collective-permute-start.5
  34.9 2.7 %collective-permute-start.6 = (f32[8,1024]{1,0:T(8,128)S(1)}, f32[8,1024]{1,0:T(8,128)S(1)}, u32[]{:S(2)}, u32[]{:S(2)}) collective-permute-start(f32[8,1024]{1,0:T(8,128)S(1)} %shard_map.133.a), channel_id=1, source_target_pairs={{0,8},{4,12},{8,0},{12,4},{1,9},{5,13},{9,1},{13,5},{2,10},{6,14},... | collective-permute-start | bytes 98312 | tf_op jit(solution)/shard_map/ppermute | solution.py:265
  37.7 1.1 collective-permute-start.7
  39.5 1.0 collective-permute-done.6.c
  40.5 2.3 %collective-permute-done.7.d = f32[8,1024]{1,0:T(8,128)S(1)} collective-permute-done((f32[8,1024]{1,0:T(8,128)S(1)}, f32[8,1024]{1,0:T(8,128)S(1)}, u32[]{:S(2)}, u32[]{:S(2)}) %collective-permute-start.7) | collective-permute-done | bytes 32800 | tf_op jit(solution)/shard_map/ppermute | solution.py:265
  42.8 0.1 shard_map.134
  42.9 3.2 %shard_map.135 = (bf16[256,256]{1,0:T(8,128)(2,1)S(1)}, bf16[256,256]{1,0:T(8,128)(2,1)S(1)}, f32[256,1024]{1,0:T(8,128)S(1)}) custom-call(s32[4]{0:T(128)S(1)} %pad_add_fusion.ids_ref, s32[1]{0:T(128)S(6)} %rem.48.order_ref, bf16[8,512,256]{2,1,0:T(8,128)(2,1)S(1)} %get-tuple-element.25.pt_ref, f32[8,512,128]{2,1,0:T(8,128)} %copy-done.1, ...), custom_call_target="tpu_custom_call" | custom-call | flops 1073741824 | bytes 3145728 | tf_op jit(solution)/shard_map/pallas_call | solution.py:325
  46.1 5.9 %collective-permute-start.24 = (bf16[256,256]{1,0:T(8,128)(2,1)S(1)}, bf16[256,256]{1,0:T(8,128)(2,1)S(1)}, u32[]{:S(2)}, u32[]{:S(2)}) collective-permute-start(bf16[256,256]{1,0:T(8,128)(2,1)S(1)} %get-tuple-element.44), channel_id=1, source_target_pairs={{0,224},{32,0},{64,32},{96,64},{128,96},{160,128},{192,160},{224,1... | collective-permute-start | bytes 393224 | tf_op jit(solution)/shard_map/ppermute | solution.py:455
  52.0 6.2 %shard_map.136 = (f32[2,512,256]{2,1,0:T(8,128)S(1)}, f32[256,1024]{1,0:T(8,128)S(1)}) custom-call(s32[4]{0:T(128)S(1)} %pad_add_fusion.ids_ref, s32[2]{0:T(128)S(1)} %compare_select_fusion.2.order_ref, bf16[8,512,256]{2,1,0:T(8,128)(2,1)S(1)} %get-tuple-element.25.pt_ref, f32[8,512,128]{2,1,0:T(8,128)} %copy-done.1, bf16[256,8192]{1,0:T(8,128)(2,1)} %p_ref.9, ...), custom_call_target="tpu_custom_call" | custom-call | flops 2147483648 | bytes 3145728 | tf_op jit(solution)/shard_map/pallas_call | solution.py:325
  58.4 3.5 %collective-permute-start.25 = (bf16[512,256]{1,0:T(8,128)(2,1)S(1)}, bf16[512,256]{1,0:T(8,128)(2,1)S(1)}, u32[]{:S(2)}, u32[]{:S(2)}) collective-permute-start(bf16[512,256]{1,0:T(8,128)(2,1)S(1)} %pad_maximum_fusion), channel_id=1, source_target_pairs={{0,224},{32,0},{64,32},{96,64},{128,96},{160,128},{192,160},{224,1... | collective-permute-start | bytes 786440 | tf_op jit(solution)/shard_map/ppermute | solution.py:461
  61.9 14.0 %shard_map.137 = (f32[5,512,256]{2,1,0:T(8,128)}, f32[256,1024]{1,0:T(8,128)S(1)}) custom-call(s32[4]{0:T(128)S(1)} %pad_add_fusion.ids_ref, s32[5]{0:T(128)S(1)} %compare_select_fusion.order_ref, bf16[8,512,256]{2,1,0:T(8,128)(2,1)S(1)} %get-tuple-element.25.pt_ref, f32[8,512,128]{2,1,0:T(8,128)} %copy-done.1, bf16[256,8192]{1,0:T(8,128)(2,1)} %p_ref.9, ...), custom_call_target="tpu_custom_call" | custom-call | flops 5368709120 | bytes 3145728 | tf_op jit(solution)/shard_map/pallas_call | solution.py:325
  75.9 0.1 collective-permute-start.29
  76.0 1.1 fusion.2
  77.2 3.3 %collective-permute-start.26 = (bf16[512,256]{1,0:T(8,128)(2,1)S(1)}, bf16[512,256]{1,0:T(8,128)(2,1)S(1)}, u32[]{:S(2)}, u32[]{:S(2)}) collective-permute-start(bf16[512,256]{1,0:T(8,128)(2,1)S(1)} %fusion.2), channel_id=1, source_target_pairs={{0,224},{32,0},{64,32},{96,64},{128,96},{160,128},{192,160},{224,1... | collective-permute-start | bytes 786440 | tf_op jit(solution)/shard_map/ppermute | solution.py:464
  80.4 3.2 %collective-permute-done.29 = bf16[512,256]{1,0:T(8,128)(2,1)S(1)} collective-permute-done((bf16[512,256]{1,0:T(8,128)(2,1)S(1)}, bf16[512,256]{1,0:T(8,128)(2,1)S(1)}, u32[]{:S(2)}, u32[]{:S(2)}) %collective-permute-start.29) | collective-permute-done | bytes 262176 | tf_op jit(solution)/shard_map/ppermute | solution.py:462
  83.6 0.7 collective-permute-done.26
  84.3 1.4 %fusion.3 = (bf16[512,256]{1,0:T(8,128)(2,1)S(1)}, bf16[512,256]{1,0:T(8,128)(2,1)S(1)}) fusion(bf16[512,256]{1,0:T(8,128)(2,1)S(1)} %collective-permute-done.26, f32[5,512,256]{2,1,0:T(8,128)} %get-tuple-element.42, bf16[512,256]{1,0:T(8,128)(2,1)S(1)} %collective-permute-done.29), kind=kLoop, calls=%fused_computation.7 | loop fusion | flops 786432 | bytes 2097152 | tf_op jit(solution)/shard_map/convert_element_type | solution.py:466
  85.7 0.1 collective-permute-start.30
  85.9 0.1 collective-permute-start.11
  86.0 3.8 %collective-permute-start.27 = (bf16[512,256]{1,0:T(8,128)(2,1)S(1)}, bf16[512,256]{1,0:T(8,128)(2,1)S(1)}, u32[]{:S(2)}, u32[]{:S(2)}) collective-permute-start(bf16[512,256]{1,0:T(8,128)(2,1)S(1)} %get-tuple-element.46), channel_id=1, source_target_pairs={{0,224},{32,0},{64,32},{96,64},{128,96},{160,128},{192,160},{224,1... | collective-permute-start | bytes 786440 | tf_op jit(solution)/shard_map/ppermute | solution.py:466
  89.7 4.1 %collective-permute-done.30 = bf16[512,256]{1,0:T(8,128)(2,1)S(1)} collective-permute-done((bf16[512,256]{1,0:T(8,128)(2,1)S(1)}, bf16[512,256]{1,0:T(8,128)(2,1)S(1)}, u32[]{:S(2)}, u32[]{:S(2)}) %collective-permute-start.30) | collective-permute-done | bytes 262176 | tf_op jit(solution)/shard_map/ppermute | solution.py:465
  93.8 1.1 fusion.1
  95.0 0.7 shard_map.139
  95.8 3.2 %collective-permute-start.12 = (bf16[64,512]{1,0:T(8,128)(2,1)S(1)}, bf16[64,512]{1,0:T(8,128)(2,1)S(1)}, u32[]{:S(2)}, u32[]{:S(2)}) collective-permute-start(bf16[64,512]{1,0:T(8,128)(2,1)S(1)} %get-tuple-element.35), channel_id=1, source_target_pairs={{0,1},{1,0},{2,3},{3,2},{4,5},{5,4},{6,7},{7,6},{8,9},{9,8},{10,11... | collective-permute-start | bytes 196616 | tf_op jit(solution)/shard_map/ppermute | solution.py:265
  99.0 1.6 %collective-permute-start.14 = (bf16[64,512]{1,0:T(8,128)(2,1)S(1)}, bf16[64,512]{1,0:T(8,128)(2,1)S(1)}, u32[]{:S(2)}, u32[]{:S(2)}) collective-permute-start(bf16[64,512]{1,0:T(8,128)(2,1)S(1)} %get-tuple-element.37), channel_id=1, source_target_pairs={{0,3},{1,2},{2,1},{3,0},{4,7},{5,6},{6,5},{7,4},{8,11},{9,10},{10,... | collective-permute-start | bytes 196616 | tf_op jit(solution)/shard_map/ppermute | solution.py:265
  100.5 0.7 collective-permute-done.12.b
  101.2 3.5 %collective-permute-done.13.c = bf16[64,512]{1,0:T(8,128)(2,1)S(1)} collective-permute-done((bf16[64,512]{1,0:T(8,128)(2,1)S(1)}, bf16[64,512]{1,0:T(8,128)(2,1)S(1)}, u32[]{:S(2)}, u32[]{:S(2)}) %collective-permute-start.13) | collective-permute-done | bytes 65568 | tf_op jit(solution)/shard_map/ppermute | solution.py:265
  104.7 0.6 shard_map.140
  105.3 0.1 collective-permute-start.15
  105.4 1.9 %collective-permute-start.16 = (bf16[16,512]{1,0:T(8,128)(2,1)S(1)}, bf16[16,512]{1,0:T(8,128)(2,1)S(1)}, u32[]{:S(2)}, u32[]{:S(2)}) collective-permute-start(bf16[16,512]{1,0:T(8,128)(2,1)S(1)} %get-tuple-element.40), channel_id=1, source_target_pairs={{0,8},{4,12},{8,0},{12,4},{1,9},{5,13},{9,1},{13,5},{2,10},{6,14},... | collective-permute-start | bytes 49160 | tf_op jit(solution)/shard_map/ppermute | solution.py:265
  107.4 2.8 %collective-permute-start.17 = (bf16[16,512]{1,0:T(8,128)(2,1)S(1)}, bf16[16,512]{1,0:T(8,128)(2,1)S(1)}, u32[]{:S(2)}, u32[]{:S(2)}) collective-permute-start(bf16[16,512]{1,0:T(8,128)(2,1)S(1)} %get-tuple-element.41), channel_id=1, source_target_pairs={{0,12},{4,8},{8,4},{12,0},{1,13},{5,9},{9,5},{13,1},{2,14},{6,10},... | collective-permute-start | bytes 49160 | tf_op jit(solution)/shard_map/ppermute | solution.py:265
  110.1 1.4 %collective-permute-start.9 = (f32[8,256]{1,0:T(8,128)S(1)}, f32[8,256]{1,0:T(8,128)S(1)}, u32[]{:S(2)}, u32[]{:S(2)}) collective-permute-start(f32[8,256]{1,0:T(8,128)S(1)} %add.48), channel_id=1, source_target_pairs={{0,64},{32,96},{64,0},{96,32},{128,192},{160,224},{192,128},{224,1... | collective-permute-start | bytes 24584 | tf_op jit(solution)/shard_map/ppermute | solution.py:265
  111.6 0.8 collective-permute-done.17.d
  112.3 0.5 collective-permute-start.18
  112.8 3.8 %collective-permute-start.19 = (bf16[16,512]{1,0:T(8,128)(2,1)S(1)}, bf16[16,512]{1,0:T(8,128)(2,1)S(1)}, u32[]{:S(2)}, u32[]{:S(2)}) collective-permute-start(bf16[16,512]{1,0:T(8,128)(2,1)S(1)} %shard_map.141.a), channel_id=1, source_target_pairs={{0,8},{4,12},{8,0},{12,4},{1,9},{5,13},{9,1},{13,5},{2,10},{6,14},... | collective-permute-start | bytes 49160 | tf_op jit(solution)/shard_map/ppermute | solution.py:265
  116.6 0.5 collective-permute-start.20
  117.1 3.7 %collective-permute-start.10 = (f32[8,256]{1,0:T(8,128)S(1)}, f32[8,256]{1,0:T(8,128)S(1)}, u32[]{:S(2)}, u32[]{:S(2)}) collective-permute-start(f32[8,256]{1,0:T(8,128)S(1)} %add.49), channel_id=1, source_target_pairs={{0,128},{32,160},{64,192},{96,224},{128,0},{160,32},{192,64},{224,... | collective-permute-start | bytes 24584 | tf_op jit(solution)/shard_map/ppermute | solution.py:265
  120.9 0.7 collective-permute-done.20.d
  121.6 0.6 shard_map.142.a
  122.2 1.5 %collective-permute-start.21 = (bf16[64,512]{1,0:T(8,128)(2,1)S(1)}, bf16[64,512]{1,0:T(8,128)(2,1)S(1)}, u32[]{:S(2)}, u32[]{:S(2)}) collective-permute-start(bf16[64,512]{1,0:T(8,128)(2,1)S(1)} %shard_map.142.a), channel_id=1, source_target_pairs={{0,1},{1,0},{2,3},{3,2},{4,5},{5,4},{6,7},{7,6},{8,9},{9,8},{10,11... | collective-permute-start | bytes 196616 | tf_op jit(solution)/shard_map/ppermute | solution.py:265
  123.6 1.9 %collective-permute-start.22 = (bf16[64,512]{1,0:T(8,128)(2,1)S(1)}, bf16[64,512]{1,0:T(8,128)(2,1)S(1)}, u32[]{:S(2)}, u32[]{:S(2)}) collective-permute-start(bf16[64,512]{1,0:T(8,128)(2,1)S(1)} %shard_map.142.a), channel_id=1, source_target_pairs={{0,2},{1,3},{2,0},{3,1},{4,6},{5,7},{6,4},{7,5},{8,10},{9,11},{10,... | collective-permute-start | bytes 196616 | tf_op jit(solution)/shard_map/ppermute | solution.py:265
  125.6 0.5 collective-permute-start.23
  126.1 0.5 slice.46
  126.6 2.4 %shard_map.144 = f32[8,8192]{1,0:T(8,128)S(1)} custom-call(f32[8,256]{1,0:T(8,128)S(1)} %add.50.misc_ref, bf16[256,8192]{1,0:T(8,128)(2,1)S(1)} %copy-done), custom_call_target="tpu_custom_call" | custom-call | flops 100663296 | bytes 5242880 | tf_op jit(solution)/shard_map/pallas_call | solution.py:414
  128.9 0.6 slice.49
  129.6 0.5 collective-permute-done.23.d
  130.1 2.9 %shard_map.143 = f32[4,256,256]{2,1,0:T(8,128)} custom-call(s32[4]{0:T(128)S(1)} %pad_add_fusion.ids_ref, s32[4]{0:T(128)S(1)} %copy-done.9, s32[4,128]{1,0:T(4,128)S(1)} %copy-done.7, bf16[4,256,256]{2,1,0:T(8,128)(2,1)S(1)} %copy-done.3, bf16[64,512]{1,0:T(8,128)(2,1)S(1)} %shard_map.142.a, bf16[64,512]{1,0:T(8,128)(2,1)S(1)} %collective-permute-done.21.b, ...), custom_call_target="tpu_custom_call" | custom-call | flops 1048576 | bytes 1048576 | tf_op jit(solution)/shard_map/pallas_call | solution.py:390
  133.0 1.9 %fusion.4 = f32[512,256]{1,0:T(8,128)} fusion(bf16[512,256]{1,0:T(8,128)(2,1)S(1)} %collective-permute-done.31, bf16[512,256]{1,0:T(8,128)(2,1)S(1)} %collective-permute-done.27, f32[5,512,256]{2,1,0:T(8,128)} %get-tuple-element.42), kind=kLoop, calls=%fused_computation.9 | loop fusion | flops 524288 | bytes 1572864 | tf_op jit(solution)/shard_map/add | solution.py:468
  (57 shorter events, 0.6 us)
Async XLA Ops:
  0.6 1.0 copy-start.2
  1.7 1.0 copy-start.4
  2.7 0.7 copy-start.6
  3.4 0.7 copy-start.8
  4.1 7.5 %copy-start.9 = (s32[4]{0:T(128)S(1)}, s32[4]{0:T(128)}, u32[]{:S(2)}) copy-start(s32[4]{0:T(128)} %count_ref.5) | copy-start | bytes 52
  5.1 6.4 %collective-permute-start = (bf16[2,512,256]{2,1,0:T(8,128)(2,1)S(1)}, bf16[2,512,256]{2,1,0:T(8,128)(2,1)S(1)}, u32[]{:S(2)}, u32[]{:S(2)}) collective-permute-start(bf16[2,512,256]{2,1,0:T(8,128)(2,1)S(1)} %shard_map.130.mine_ref), channel_id=1, source_target_pairs={{0,16},{16,0},{1,17},{17,1},{2,18},{18,2},{3,19},{19,3},{4,20},{20... | collective-permute-start | bytes 1572872 | tf_op jit(solution)/shard_map/ppermute | solution.py:265
  5.3 0.8 copy-start.5
  11.6 13.2 %copy-start.1 = (f32[8,512,128]{2,1,0:T(8,128)}, f32[8,512,128]{2,1,0:T(8,128)S(1)}, u32[]{:S(2)}) copy-start(f32[8,512,128]{2,1,0:T(8,128)S(1)} %get-tuple-element.26.cb_ref) | copy-start | bytes 6291460
  11.6 18.5 %copy-start.11 = (s32[2]{0:T(128)S(1)}, s32[2]{0:T(128)}, u32[]{:S(2)}) copy-start(s32[2]{0:T(128)} %constant.41.clone) | copy-start | bytes 28
  11.6 27.2 %copy-start.10 = (s32[5]{0:T(128)S(1)}, s32[5]{0:T(128)}, u32[]{:S(2)}) copy-start(s32[5]{0:T(128)} %constant.42.clone) | copy-start | bytes 64
  24.8 1.4 %collective-permute-start.1 = (f32[8,1024]{1,0:T(8,128)S(1)}, f32[8,1024]{1,0:T(8,128)S(1)}, u32[]{:S(2)}, u32[]{:S(2)}) collective-permute-start(f32[8,1024]{1,0:T(8,128)S(1)} %get-tuple-element.27.mine_ref), channel_id=1, source_target_pairs={{0,16},{16,0},{1,17},{17,1},{2,18},{18,2},{3,19},{19,3},{4,20},{20... | collective-permute-start | bytes 98312 | tf_op jit(solution)/shard_map/ppermute | solution.py:265
  26.3 4.2 %collective-permute-start.2 = (f32[8,1024]{1,0:T(8,128)S(1)}, f32[8,1024]{1,0:T(8,128)S(1)}, u32[]{:S(2)}, u32[]{:S(2)}) collective-permute-start(f32[8,1024]{1,0:T(8,128)S(1)} %shard_map.132.refs_0_), channel_id=1, source_target_pairs={{0,1},{1,0},{2,3},{3,2},{4,5},{5,4},{6,7},{7,6},{8,9},{9,8},{10,11... | collective-permute-start | bytes 98312 | tf_op jit(solution)/shard_map/ppermute | solution.py:265
  28.5 5.4 %collective-permute-start.3 = (f32[8,1024]{1,0:T(8,128)S(1)}, f32[8,1024]{1,0:T(8,128)S(1)}, u32[]{:S(2)}, u32[]{:S(2)}) collective-permute-start(f32[8,1024]{1,0:T(8,128)S(1)} %shard_map.132.refs_0_), channel_id=1, source_target_pairs={{0,2},{1,3},{2,0},{3,1},{4,6},{5,7},{6,4},{7,5},{8,10},{9,11},{10,... | collective-permute-start | bytes 98312 | tf_op jit(solution)/shard_map/ppermute | solution.py:265
  29.4 4.6 %collective-permute-start.4 = (f32[8,1024]{1,0:T(8,128)S(1)}, f32[8,1024]{1,0:T(8,128)S(1)}, u32[]{:S(2)}, u32[]{:S(2)}) collective-permute-start(f32[8,1024]{1,0:T(8,128)S(1)} %shard_map.132.refs_0_), channel_id=1, source_target_pairs={{0,3},{1,2},{2,1},{3,0},{4,7},{5,6},{6,5},{7,4},{8,11},{9,10},{10,... | collective-permute-start | bytes 98312 | tf_op jit(solution)/shard_map/ppermute | solution.py:265
  34.0 5.5 %collective-permute-start.5 = (f32[8,1024]{1,0:T(8,128)S(1)}, f32[8,1024]{1,0:T(8,128)S(1)}, u32[]{:S(2)}, u32[]{:S(2)}) collective-permute-start(f32[8,1024]{1,0:T(8,128)S(1)} %shard_map.133.a), channel_id=1, source_target_pairs={{0,4},{4,0},{8,12},{12,8},{1,5},{5,1},{9,13},{13,9},{2,6},{6,2},{1... | collective-permute-start | bytes 98312 | tf_op jit(solution)/shard_map/ppermute | solution.py:265
  34.9 5.5 %collective-permute-start.6 = (f32[8,1024]{1,0:T(8,128)S(1)}, f32[8,1024]{1,0:T(8,128)S(1)}, u32[]{:S(2)}, u32[]{:S(2)}) collective-permute-start(f32[8,1024]{1,0:T(8,128)S(1)} %shard_map.133.a), channel_id=1, source_target_pairs={{0,8},{4,12},{8,0},{12,4},{1,9},{5,13},{9,1},{13,5},{2,10},{6,14},... | collective-permute-start | bytes 98312 | tf_op jit(solution)/shard_map/ppermute | solution.py:265
  37.7 5.1 %collective-permute-start.7 = (f32[8,1024]{1,0:T(8,128)S(1)}, f32[8,1024]{1,0:T(8,128)S(1)}, u32[]{:S(2)}, u32[]{:S(2)}) collective-permute-start(f32[8,1024]{1,0:T(8,128)S(1)} %shard_map.133.a), channel_id=1, source_target_pairs={{0,12},{4,8},{8,4},{12,0},{1,13},{5,9},{9,5},{13,1},{2,14},{6,10},... | collective-permute-start | bytes 98312 | tf_op jit(solution)/shard_map/ppermute | solution.py:265
  46.1 12.2 %collective-permute-start.24 = (bf16[256,256]{1,0:T(8,128)(2,1)S(1)}, bf16[256,256]{1,0:T(8,128)(2,1)S(1)}, u32[]{:S(2)}, u32[]{:S(2)}) collective-permute-start(bf16[256,256]{1,0:T(8,128)(2,1)S(1)} %get-tuple-element.44), channel_id=1, source_target_pairs={{0,224},{32,0},{64,32},{96,64},{128,96},{160,128},{192,160},{224,1... | collective-permute-start | bytes 393224 | tf_op jit(solution)/shard_map/ppermute | solution.py:455
  52.0 6.3 %collective-permute-start.28 = (bf16[256,256]{1,0:T(8,128)(2,1)S(1)}, bf16[256,256]{1,0:T(8,128)(2,1)S(1)}, u32[]{:S(2)}, u32[]{:S(2)}) collective-permute-start(bf16[256,256]{1,0:T(8,128)(2,1)S(1)} %get-tuple-element.45), channel_id=1, source_target_pairs={{0,32},{32,64},{64,96},{96,128},{128,160},{160,192},{192,224},{224... | collective-permute-start | bytes 393224 | tf_op jit(solution)/shard_map/ppermute | solution.py:456
  58.4 17.6 %collective-permute-start.25 = (bf16[512,256]{1,0:T(8,128)(2,1)S(1)}, bf16[512,256]{1,0:T(8,128)(2,1)S(1)}, u32[]{:S(2)}, u32[]{:S(2)}) collective-permute-start(bf16[512,256]{1,0:T(8,128)(2,1)S(1)} %pad_maximum_fusion), channel_id=1, source_target_pairs={{0,224},{32,0},{64,32},{96,64},{128,96},{160,128},{192,160},{224,1... | collective-permute-start | bytes 786440 | tf_op jit(solution)/shard_map/ppermute | solution.py:461
  75.9 7.7 %collective-permute-start.29 = (bf16[512,256]{1,0:T(8,128)(2,1)S(1)}, bf16[512,256]{1,0:T(8,128)(2,1)S(1)}, u32[]{:S(2)}, u32[]{:S(2)}) collective-permute-start(bf16[512,256]{1,0:T(8,128)(2,1)S(1)} %pad_maximum_fusion.1), channel_id=1, source_target_pairs={{0,32},{32,64},{64,96},{96,128},{128,160},{160,192},{192,224},{224... | collective-permute-start | bytes 786440 | tf_op jit(solution)/shard_map/ppermute | solution.py:462
  77.2 7.2 %collective-permute-start.26 = (bf16[512,256]{1,0:T(8,128)(2,1)S(1)}, bf16[512,256]{1,0:T(8,128)(2,1)S(1)}, u32[]{:S(2)}, u32[]{:S(2)}) collective-permute-start(bf16[512,256]{1,0:T(8,128)(2,1)S(1)} %fusion.2), channel_id=1, source_target_pairs={{0,224},{32,0},{64,32},{96,64},{128,96},{160,128},{192,160},{224,1... | collective-permute-start | bytes 786440 | tf_op jit(solution)/shard_map/ppermute | solution.py:464
  85.7 8.1 %collective-permute-start.30 = (bf16[512,256]{1,0:T(8,128)(2,1)S(1)}, bf16[512,256]{1,0:T(8,128)(2,1)S(1)}, u32[]{:S(2)}, u32[]{:S(2)}) collective-permute-start(bf16[512,256]{1,0:T(8,128)(2,1)S(1)} %get-tuple-element.47), channel_id=1, source_target_pairs={{0,32},{32,64},{64,96},{96,128},{128,160},{160,192},{192,224},{224... | collective-permute-start | bytes 786440 | tf_op jit(solution)/shard_map/ppermute | solution.py:465
  85.9 40.7 %copy-start = (bf16[256,8192]{1,0:T(8,128)(2,1)S(1)}, bf16[256,8192]{1,0:T(8,128)(2,1)}, u32[]{:S(2)}) copy-start(bf16[256,8192]{1,0:T(8,128)(2,1)} %p_ref.9) | copy-start | bytes 12582916
  85.9 9.1 %collective-permute-start.11 = (bf16[256,512]{1,0:T(8,128)(2,1)S(1)}, bf16[256,512]{1,0:T(8,128)(2,1)S(1)}, u32[]{:S(2)}, u32[]{:S(2)}) collective-permute-start(bf16[256,512]{1,0:T(8,128)(2,1)S(1)} %shard_map.138), channel_id=1, source_target_pairs={{0,16},{16,0},{1,17},{17,1},{2,18},{18,2},{3,19},{19,3},{4,20},{20... | collective-permute-start | bytes 786440 | tf_op jit(solution)/shard_map/ppermute | solution.py:265
  86.0 47.0 %collective-permute-start.27 = (bf16[512,256]{1,0:T(8,128)(2,1)S(1)}, bf16[512,256]{1,0:T(8,128)(2,1)S(1)}, u32[]{:S(2)}, u32[]{:S(2)}) collective-permute-start(bf16[512,256]{1,0:T(8,128)(2,1)S(1)} %get-tuple-element.46), channel_id=1, source_target_pairs={{0,224},{32,0},{64,32},{96,64},{128,96},{160,128},{192,160},{224,1... | collective-permute-start | bytes 786440 | tf_op jit(solution)/shard_map/ppermute | solution.py:466
  94.9 38.1 %collective-permute-start.31 = (bf16[512,256]{1,0:T(8,128)(2,1)S(1)}, bf16[512,256]{1,0:T(8,128)(2,1)S(1)}, u32[]{:S(2)}, u32[]{:S(2)}) collective-permute-start(bf16[512,256]{1,0:T(8,128)(2,1)S(1)} %fusion.1), channel_id=1, source_target_pairs={{0,32},{32,64},{64,96},{96,128},{128,160},{160,192},{192,224},{224... | collective-permute-start | bytes 786440 | tf_op jit(solution)/shard_map/ppermute | solution.py:467
  95.8 34.3 %copy-start.3 = (bf16[4,256,256]{2,1,0:T(8,128)(2,1)S(1)}, bf16[4,256,256]{2,1,0:T(8,128)(2,1)}, u32[]{:S(2)}) copy-start(bf16[4,256,256]{2,1,0:T(8,128)(2,1)} %s_ref.3) | copy-start | bytes 1572868
  95.8 34.3 %copy-start.7 = (s32[4,128]{1,0:T(4,128)S(1)}, s32[4,128]{1,0:T(4,128)}, u32[]{:S(2)}) copy-start(s32[4,128]{1,0:T(4,128)} %index_ref.3) | copy-start | bytes 6148
  95.8 5.4 %collective-permute-start.12 = (bf16[64,512]{1,0:T(8,128)(2,1)S(1)}, bf16[64,512]{1,0:T(8,128)(2,1)S(1)}, u32[]{:S(2)}, u32[]{:S(2)}) collective-permute-start(bf16[64,512]{1,0:T(8,128)(2,1)S(1)} %get-tuple-element.35), channel_id=1, source_target_pairs={{0,1},{1,0},{2,3},{3,2},{4,5},{5,4},{6,7},{7,6},{8,9},{9,8},{10,11... | collective-permute-start | bytes 196616 | tf_op jit(solution)/shard_map/ppermute | solution.py:265
  99.0 5.8 %collective-permute-start.13 = (bf16[64,512]{1,0:T(8,128)(2,1)S(1)}, bf16[64,512]{1,0:T(8,128)(2,1)S(1)}, u32[]{:S(2)}, u32[]{:S(2)}) collective-permute-start(bf16[64,512]{1,0:T(8,128)(2,1)S(1)} %get-tuple-element.36), channel_id=1, source_target_pairs={{0,2},{1,3},{2,0},{3,1},{4,6},{5,7},{6,4},{7,5},{8,10},{9,11},{10,... | collective-permute-start | bytes 196616 | tf_op jit(solution)/shard_map/ppermute | solution.py:265
  99.0 5.8 %collective-permute-start.14 = (bf16[64,512]{1,0:T(8,128)(2,1)S(1)}, bf16[64,512]{1,0:T(8,128)(2,1)S(1)}, u32[]{:S(2)}, u32[]{:S(2)}) collective-permute-start(bf16[64,512]{1,0:T(8,128)(2,1)S(1)} %get-tuple-element.37), channel_id=1, source_target_pairs={{0,3},{1,2},{2,1},{3,0},{4,7},{5,6},{6,5},{7,4},{8,11},{9,10},{10,... | collective-permute-start | bytes 196616 | tf_op jit(solution)/shard_map/ppermute | solution.py:265
  101.2 6.2 %collective-permute-start.8 = (f32[8,256]{1,0:T(8,128)S(1)}, f32[8,256]{1,0:T(8,128)S(1)}, u32[]{:S(2)}, u32[]{:S(2)}) collective-permute-start(f32[8,256]{1,0:T(8,128)S(1)} %get-tuple-element.29), channel_id=1, source_target_pairs={{0,32},{32,0},{64,96},{96,64},{128,160},{160,128},{192,224},{224,1... | collective-permute-start | bytes 24584 | tf_op jit(solution)/shard_map/ppermute | solution.py:265
  105.3 4.8 %collective-permute-start.15 = (bf16[16,512]{1,0:T(8,128)(2,1)S(1)}, bf16[16,512]{1,0:T(8,128)(2,1)S(1)}, u32[]{:S(2)}, u32[]{:S(2)}) collective-permute-start(bf16[16,512]{1,0:T(8,128)(2,1)S(1)} %get-tuple-element.39), channel_id=1, source_target_pairs={{0,4},{4,0},{8,12},{12,8},{1,5},{5,1},{9,13},{13,9},{2,6},{6,2},{1... | collective-permute-start | bytes 49160 | tf_op jit(solution)/shard_map/ppermute | solution.py:265
  105.4 6.1 %collective-permute-start.16 = (bf16[16,512]{1,0:T(8,128)(2,1)S(1)}, bf16[16,512]{1,0:T(8,128)(2,1)S(1)}, u32[]{:S(2)}, u32[]{:S(2)}) collective-permute-start(bf16[16,512]{1,0:T(8,128)(2,1)S(1)} %get-tuple-element.40), channel_id=1, source_target_pairs={{0,8},{4,12},{8,0},{12,4},{1,9},{5,13},{9,1},{13,5},{2,10},{6,14},... | collective-permute-start | bytes 49160 | tf_op jit(solution)/shard_map/ppermute | solution.py:265
  107.4 5.0 %collective-permute-start.17 = (bf16[16,512]{1,0:T(8,128)(2,1)S(1)}, bf16[16,512]{1,0:T(8,128)(2,1)S(1)}, u32[]{:S(2)}, u32[]{:S(2)}) collective-permute-start(bf16[16,512]{1,0:T(8,128)(2,1)S(1)} %get-tuple-element.41), channel_id=1, source_target_pairs={{0,12},{4,8},{8,4},{12,0},{1,13},{5,9},{9,5},{13,1},{2,14},{6,10},... | collective-permute-start | bytes 49160 | tf_op jit(solution)/shard_map/ppermute | solution.py:265
  110.1 6.5 %collective-permute-start.9 = (f32[8,256]{1,0:T(8,128)S(1)}, f32[8,256]{1,0:T(8,128)S(1)}, u32[]{:S(2)}, u32[]{:S(2)}) collective-permute-start(f32[8,256]{1,0:T(8,128)S(1)} %add.48), channel_id=1, source_target_pairs={{0,64},{32,96},{64,0},{96,32},{128,192},{160,224},{192,128},{224,1... | collective-permute-start | bytes 24584 | tf_op jit(solution)/shard_map/ppermute | solution.py:265
  112.3 4.8 %collective-permute-start.18 = (bf16[16,512]{1,0:T(8,128)(2,1)S(1)}, bf16[16,512]{1,0:T(8,128)(2,1)S(1)}, u32[]{:S(2)}, u32[]{:S(2)}) collective-permute-start(bf16[16,512]{1,0:T(8,128)(2,1)S(1)} %shard_map.141.a), channel_id=1, source_target_pairs={{0,4},{4,0},{8,12},{12,8},{1,5},{5,1},{9,13},{13,9},{2,6},{6,2},{1... | collective-permute-start | bytes 49160 | tf_op jit(solution)/shard_map/ppermute | solution.py:265
  112.8 8.1 %collective-permute-start.19 = (bf16[16,512]{1,0:T(8,128)(2,1)S(1)}, bf16[16,512]{1,0:T(8,128)(2,1)S(1)}, u32[]{:S(2)}, u32[]{:S(2)}) collective-permute-start(bf16[16,512]{1,0:T(8,128)(2,1)S(1)} %shard_map.141.a), channel_id=1, source_target_pairs={{0,8},{4,12},{8,0},{12,4},{1,9},{5,13},{9,1},{13,5},{2,10},{6,14},... | collective-permute-start | bytes 49160 | tf_op jit(solution)/shard_map/ppermute | solution.py:265
  116.6 5.0 %collective-permute-start.20 = (bf16[16,512]{1,0:T(8,128)(2,1)S(1)}, bf16[16,512]{1,0:T(8,128)(2,1)S(1)}, u32[]{:S(2)}, u32[]{:S(2)}) collective-permute-start(bf16[16,512]{1,0:T(8,128)(2,1)S(1)} %shard_map.141.a), channel_id=1, source_target_pairs={{0,12},{4,8},{8,4},{12,0},{1,13},{5,9},{9,5},{13,1},{2,14},{6,10},... | collective-permute-start | bytes 49160 | tf_op jit(solution)/shard_map/ppermute | solution.py:265
  117.1 8.5 %collective-permute-start.10 = (f32[8,256]{1,0:T(8,128)S(1)}, f32[8,256]{1,0:T(8,128)S(1)}, u32[]{:S(2)}, u32[]{:S(2)}) collective-permute-start(f32[8,256]{1,0:T(8,128)S(1)} %add.49), channel_id=1, source_target_pairs={{0,128},{32,160},{64,192},{96,224},{128,0},{160,32},{192,64},{224,... | collective-permute-start | bytes 24584 | tf_op jit(solution)/shard_map/ppermute | solution.py:265
  122.2 7.4 %collective-permute-start.21 = (bf16[64,512]{1,0:T(8,128)(2,1)S(1)}, bf16[64,512]{1,0:T(8,128)(2,1)S(1)}, u32[]{:S(2)}, u32[]{:S(2)}) collective-permute-start(bf16[64,512]{1,0:T(8,128)(2,1)S(1)} %shard_map.142.a), channel_id=1, source_target_pairs={{0,1},{1,0},{2,3},{3,2},{4,5},{5,4},{6,7},{7,6},{8,9},{9,8},{10,11... | collective-permute-start | bytes 196616 | tf_op jit(solution)/shard_map/ppermute | solution.py:265
  123.6 6.0 %collective-permute-start.22 = (bf16[64,512]{1,0:T(8,128)(2,1)S(1)}, bf16[64,512]{1,0:T(8,128)(2,1)S(1)}, u32[]{:S(2)}, u32[]{:S(2)}) collective-permute-start(bf16[64,512]{1,0:T(8,128)(2,1)S(1)} %shard_map.142.a), channel_id=1, source_target_pairs={{0,2},{1,3},{2,0},{3,1},{4,6},{5,7},{6,4},{7,5},{8,10},{9,11},{10,... | collective-permute-start | bytes 196616 | tf_op jit(solution)/shard_map/ppermute | solution.py:265
  125.6 4.5 %collective-permute-start.23 = (bf16[64,512]{1,0:T(8,128)(2,1)S(1)}, bf16[64,512]{1,0:T(8,128)(2,1)S(1)}, u32[]{:S(2)}, u32[]{:S(2)}) collective-permute-start(bf16[64,512]{1,0:T(8,128)(2,1)S(1)} %shard_map.142.a), channel_id=1, source_target_pairs={{0,3},{1,2},{2,1},{3,0},{4,7},{5,6},{6,5},{7,4},{8,11},{9,10},{10,... | collective-permute-start | bytes 196616 | tf_op jit(solution)/shard_map/ppermute | solution.py:265

commit v2 on v1

v2 whole, which is shorter than its diff:
```python
import functools
import math

import jax
import jax.numpy as jnp
from jax import lax
from jax.experimental import pallas as pl
from jax.experimental.pallas import tpu as pltpu
from jax.sharding import Mesh, PartitionSpec as P

bf16 = jnp.bfloat16
f32 = jnp.float32
log2e = math.log2(math.e)
ln2 = math.log(2.0)
t_scale = log2e / 0.04
s_scale = log2e / 0.1
inverse_temp = 10.0
norm_epsilon = 1e-06
low = -1e30

Z, CORES, X, Y = 8, 2, 4, 4
D = 256
SLOTS = 128
IMAGES = 64
TOTAL = 4096
LOCAL = 4
ROWS = LOCAL * SLOTS
BOTH = 2 * ROWS
CHUNK = 512
TILE = 256
EXTRA = 48

NT = (((1,), (1,)), ((), ()))
TN = (((0,), (0,)), ((), ()))


def dot(a, b, dims=(((1,), (0,)), ((), ()))):
    return lax.dot_general(a, b, dims, preferred_element_type=f32)


def params():
    return pltpu.CompilerParams(vmem_limit_bytes=48 * 1024 * 1024)


def cost(flops, nbytes, trans=0):
    return pl.CostEstimate(flops=flops, bytes_accessed=nbytes, transcendentals=trans)


def picks(index_ref, count, i):
    patch = lax.broadcasted_iota(jnp.int32, (D, SLOTS), 0)
    slot = lax.broadcasted_iota(jnp.int32, (D, SLOTS), 1)
    hit = (patch == index_ref[i : i + 1, :]) & (slot < count)
    return jnp.where(hit, 1.0, 0.0).astype(bf16)


def unit_rows(values):
    length = jnp.sqrt(jnp.sum(values * values, axis=1, keepdims=True) + norm_epsilon)
    return values / length, length


def prep_kernel(count_ref, index_ref, s_ref, t_ref, out_ref):
    for i in range(LOCAL):
        pick = picks(index_ref, count_ref[i], i)
        for which, ref in enumerate((s_ref, t_ref)):
            unit, _ = unit_rows(dot(pick, ref[i], TN))
            out_ref[which, i * SLOTS : (i + 1) * SLOTS, :] = unit.astype(bf16)


def prep(count, index, student, teacher):
    smem = pl.BlockSpec(memory_space=pltpu.SMEM)
    vmem = pl.BlockSpec(memory_space=pltpu.VMEM)
    return pl.pallas_call(
        prep_kernel,
        out_shape=jax.ShapeDtypeStruct((2, ROWS, D), bf16),
        in_specs=[smem, vmem, vmem, vmem],
        out_specs=vmem,
        compiler_params=params(),
        cost_estimate=cost(2 * 2 * ROWS * D * D, 1 << 21),
    )(count, index, student, teacher)


def wide(block, times):
    return jnp.concatenate([block] * times, axis=1)


def stats_kernel(ids_ref, p_ref, c_ref, mine_ref, other_ref, out_ref, sum_ref, pt_ref, cb_ref, acc):
    step = pl.program_id(0)

    @pl.when(step == 0)
    def _():
        acc[...] = jnp.zeros(acc.shape, f32)
        acc[0] = jnp.full((8, BOTH), low, f32)
        acc[3] = jnp.full((8, BOTH), low, f32)

    protos = p_ref[...].T
    pt_ref[0] = protos
    column = jnp.broadcast_to(c_ref[0] * -t_scale, (128, CHUNK)).T
    cb_ref[0] = column
    shift = wide(column, TILE // 128)
    for half, ref in enumerate((mine_ref, other_ref)):
        for j in range(ROWS // TILE):
            rows = slice(j * TILE, (j + 1) * TILE)
            at = slice(half * ROWS + j * TILE, half * ROWS + (j + 1) * TILE)
            t_arg = (dot(protos, ref[1, rows, :], NT) * t_scale + shift).reshape(CHUNK // 8, 8, TILE)
            s_arg = (dot(protos, ref[0, rows, :], NT) * s_scale).reshape(CHUNK // 8, 8, TILE)
            t_old, s_old = acc[0, :, at], acc[3, :, at]
            t_top = jnp.maximum(t_old, jnp.max(t_arg, axis=0))
            s_top = jnp.maximum(s_old, jnp.max(s_arg, axis=0))
            t_exp = jnp.exp2(t_arg - t_top[None])
            s_exp = jnp.exp2(s_arg - s_top[None])
            t_keep = jnp.exp2(t_old - t_top)
            s_keep = jnp.exp2(s_old - s_top)
            acc[0, :, at] = t_top
            acc[1, :, at] = acc[1, :, at] * t_keep + jnp.sum(t_exp, axis=0)
            acc[2, :, at] = acc[2, :, at] * t_keep + jnp.sum(t_exp * s_arg, axis=0)
            acc[3, :, at] = s_top
            acc[4, :, at] = acc[4, :, at] * s_keep + jnp.sum(s_exp, axis=0)

    @pl.when(step == Z - 1)
    def _():
        t_top = jnp.max(acc[0], axis=0, keepdims=True)
        s_top = jnp.max(acc[3], axis=0, keepdims=True)
        t_keep = jnp.exp2(acc[0] - t_top)
        s_keep = jnp.exp2(acc[3] - s_top)
        out_ref[0:1, :] = t_top
        out_ref[1:2, :] = jnp.sum(acc[1] * t_keep, axis=0, keepdims=True)
        out_ref[2:3, :] = jnp.sum(acc[2] * t_keep, axis=0, keepdims=True)
        out_ref[3:4, :] = s_top
        out_ref[4:5, :] = jnp.sum(acc[4] * s_keep, axis=0, keepdims=True)
        out_ref[5:8, :] = jnp.zeros((3, BOTH), f32)
        slot = lax.broadcasted_iota(jnp.int32, (1, SLOTS), 1)
        for i in range(LOCAL):
            count = jnp.full((1, SLOTS), ids_ref[4 + i], jnp.int32)
            weight = 1.0 / (IMAGES * jnp.maximum(count, 1).astype(f32))
            out_ref[5:6, i * SLOTS : (i + 1) * SLOTS] = jnp.where(slot < count, weight, 0.0)
        first = jnp.sum(mine_ref[1].astype(f32), axis=0, keepdims=True)
        second = jnp.sum(other_ref[1].astype(f32), axis=0, keepdims=True)
        sum_ref[...] = jnp.broadcast_to(first + second, (8, D))


def local_stats(ids, prototypes, center, mine, other):
    whole = pl.BlockSpec((2, ROWS, D), lambda i, ids: (0, 0, 0))
    grid = pltpu.PrefetchScalarGridSpec(
        num_scalar_prefetch=1,
        grid=(Z,),
        in_specs=[
            pl.BlockSpec((D, CHUNK), lambda i, ids: (0, 2 * i + ids[1])),
            pl.BlockSpec((1, 1, CHUNK), lambda i, ids: (2 * i + ids[1], 0, 0)),
            whole,
            whole,
        ],
        out_specs=[
            pl.BlockSpec((8, BOTH), lambda i, ids: (0, 0)),
            pl.BlockSpec((8, D), lambda i, ids: (0, 0)),
            pl.BlockSpec((1, CHUNK, D), lambda i, ids: (i, 0, 0)),
            pl.BlockSpec((1, CHUNK, 128), lambda i, ids: (i, 0, 0)),
        ],
        scratch_shapes=[pltpu.VMEM((5, 8, BOTH), f32)],
    )
    return pl.pallas_call(
        stats_kernel,
        grid_spec=grid,
        out_shape=[
            jax.ShapeDtypeStruct((8, BOTH), f32),
            jax.ShapeDtypeStruct((8, D), f32),
            jax.ShapeDtypeStruct((Z, CHUNK, D), bf16),
            jax.ShapeDtypeStruct((Z, CHUNK, 128), f32),
        ],
        compiler_params=params(),
        cost_estimate=cost(4 * BOTH * Z * CHUNK * D, 6 << 20, 2 * BOTH * Z * CHUNK),
    )(ids, prototypes, center.reshape(2 * Z, 1, CHUNK), mine, other)


def split3(value):
    top = value.astype(bf16)
    rest = value - top.astype(f32)
    middle = rest.astype(bf16)
    return top, middle, (rest - middle.astype(f32)).astype(bf16)


def tree(parts):
    while len(parts) > 1:
        parts = [parts[i] + parts[i + 1] for i in range(0, len(parts), 2)]
    return parts[0]


def merged(parts):
    t_top = functools.reduce(jnp.maximum, [p[0:1] for p in parts])
    s_top = functools.reduce(jnp.maximum, [p[3:4] for p in parts])
    t_keep = [jnp.exp2(p[0:1] - t_top) for p in parts]
    s_keep = [jnp.exp2(p[3:4] - s_top) for p in parts]
    t_sum = tree([p[1:2] * k for p, k in zip(parts, t_keep)])
    cross = tree([p[2:3] * k for p, k in zip(parts, t_keep)])
    s_sum = tree([p[4:5] * k for p, k in zip(parts, s_keep)])
    return t_top, t_sum, cross, s_top, s_sum


def core_merge_kernel(mine_ref, got_ref, out_ref):
    mine = mine_ref[...]
    got = jnp.concatenate([got_ref[:, ROWS:], got_ref[:, :ROWS]], axis=1)
    for i, row in enumerate(merged([mine, got])):
        out_ref[i : i + 1, :] = row
    out_ref[5:6, :] = mine[5:6] + got[5:6]
    out_ref[6:8, :] = jnp.zeros((2, BOTH), f32)


def merge_kernel(*refs):
    out_ref = refs[-1]
    parts = [ref[...] for ref in refs[:-1]]
    for i, row in enumerate(merged(parts)):
        out_ref[i : i + 1, :] = row
    out_ref[5:8, :] = parts[0][5:8]


def last_merge_kernel(scale_ref, ids_ref, a, b, c, d, sum_ref, coef_ref, misc_ref):
    parts = [ref[...] for ref in (a, b, c, d)]
    t_top, t_sum, cross, s_top, s_sum = merged(parts)
    weight = parts[0][5:6]
    live = weight > 0.0
    s_lse = s_top + jnp.log2(s_sum)
    ce = (s_lse - cross / t_sum) * ln2
    factor = jnp.log2(jnp.where(live, weight * (scale_ref[0] * inverse_temp), 1.0))
    coef_ref[0:1, :] = jnp.where(live, factor - s_lse, low)
    coef_ref[1:2, :] = jnp.where(live, factor - t_top - jnp.log2(t_sum), low)
    coef_ref[2:8, :] = jnp.zeros((6, BOTH), f32)
    part = jnp.where(live, weight * ce, 0.0)
    first = jnp.sum(part[:, :ROWS], axis=1, keepdims=True)
    second = jnp.sum(part[:, ROWS:], axis=1, keepdims=True)
    slot = lax.broadcasted_iota(jnp.int32, (EXTRA, D), 0)
    mine = jnp.bitwise_and(slot, Z - 1) == ids_ref[0]
    row_sum = split3(sum_ref[0:1, :])
    losses = split3(jnp.broadcast_to(first + second, (1, D)))
    block = jnp.zeros((EXTRA, D), f32)
    for i in range(3):
        block = jnp.where(slot // Z == i, row_sum[i].astype(f32), block)
        block = jnp.where(slot // Z == 3 + i, losses[i].astype(f32), block)
    misc_ref[...] = jnp.where(mine, block, 0.0).astype(bf16)


def small_call(kernel, out_shape, *args, smem=()):
    specs = [
        pl.BlockSpec(memory_space=pltpu.SMEM if i in smem else pltpu.VMEM) for i in range(len(args))
    ]
    vmem = pl.BlockSpec(memory_space=pltpu.VMEM)
    return pl.pallas_call(
        kernel,
        out_shape=out_shape,
        in_specs=specs,
        out_specs=jax.tree.map(lambda _: vmem, out_shape),
        compiler_params=params(),
        cost_estimate=cost(1 << 20, 1 << 18),
    )(*args)


def swapped(axis, size, bit):
    return [(i, i ^ bit) for i in range(size)]


def swap(value, axis, size, bit):
    return lax.ppermute(value, axis, swapped(axis, size, bit))


def grad_kernel(n, split, ids_ref, order_ref, pt_ref, cb_ref, p_ref, mine_ref, other_ref, coef_ref, misc_ref, *refs):
    out_refs, du_ref = refs[:-1], refs[-1]
    step = pl.program_id(0)
    protos = pt_ref[0]
    shift = wide(cb_ref[0], TILE // 128)
    wide_p = p_ref[...]
    total = None

    @pl.when(step == 0)
    def _():
        du_ref[...] = jnp.zeros((D, BOTH), f32)

    for half, ref in enumerate((mine_ref, other_ref)):
        for j in range(ROWS // TILE):
            rows = slice(j * TILE, (j + 1) * TILE)
            at = slice(half * ROWS + j * TILE, half * ROWS + (j + 1) * TILE)
            s_rows = ref[0, rows, :]
            t_arg = dot(protos, ref[1, rows, :], NT) * t_scale + shift + coef_ref[1:2, at]
            s_arg = dot(protos, s_rows, NT) * s_scale + coef_ref[0:1, at]
            dlogit = (jnp.exp2(s_arg) - jnp.exp2(t_arg)).astype(bf16)
            part = dot(dlogit, s_rows)
            total = part if total is None else total + part
            du_ref[:, at] += dot(wide_p, dlogit)

    if split:
        half = CHUNK // 2
        out_refs[0][:half, :] = total[:half].astype(bf16)
        out_refs[0][half:, :] = misc_ref[...]
        out_refs[1][...] = total[half:].astype(bf16)
    else:
        for i in range(n):

            @pl.when(step == i)
            def _(i=i):
                out_refs[i][...] = total


def grads(ids, offsets, split, turned, shifts, prototypes, mine, other, coef, misc):
    n = len(offsets)
    order = lax.rem(ids[0] + jnp.array([d % Z for d in offsets], jnp.int32), Z)
    whole = pl.BlockSpec((2, ROWS, D), lambda i, ids, order: (0, 0, 0))
    if split:
        shapes = [(CHUNK // 2 + EXTRA, D), (CHUNK // 2, D)]
        outs = [jax.ShapeDtypeStruct(shape, bf16) for shape in shapes]
    else:
        outs = [jax.ShapeDtypeStruct((CHUNK, D), f32)] * n
    specs = [pl.BlockSpec(out.shape, lambda i, ids, order: (0, 0)) for out in outs]
    grid = pltpu.PrefetchScalarGridSpec(
        num_scalar_prefetch=2,
        grid=(n,),
        in_specs=[
            pl.BlockSpec((1, CHUNK, D), lambda i, ids, order: (order[i], 0, 0)),
            pl.BlockSpec((1, CHUNK, 128), lambda i, ids, order: (order[i], 0, 0)),
            pl.BlockSpec((D, CHUNK), lambda i, ids, order: (0, 2 * order[i] + ids[1])),
            whole,
            whole,
            pl.BlockSpec((8, BOTH), lambda i, ids, order: (0, 0)),
            pl.BlockSpec((EXTRA, D), lambda i, ids, order: (0, 0)),
        ],
        out_specs=specs + [pl.BlockSpec((D, BOTH), lambda i, ids, order: (0, 0))],
    )
    return pl.pallas_call(
        functools.partial(grad_kernel, n, split),
        grid_spec=grid,
        out_shape=outs + [jax.ShapeDtypeStruct((D, BOTH), f32)],
        compiler_params=params(),
        cost_estimate=cost(8 * BOTH * n * CHUNK * D, 3 << 20, 2 * BOTH * n * CHUNK),
    )(ids, order, turned, shifts, prototypes, mine, other, coef, misc)


def du_send_kernel(ids_ref, a, b, c, out_ref):
    total = (a[...] + b[...] + c[...]).astype(bf16)
    core = ids_ref[1]
    out_ref[core] = total[:, :ROWS]
    out_ref[1 - core] = total[:, ROWS:]


def du_sum_kernel(got_ref, out_ref):
    total = jnp.sum(got_ref[...].astype(f32), axis=0).astype(bf16)
    out_ref[...] = jnp.broadcast_to(total[None], (X * Y,) + total.shape)


def halves_kernel(offset, with_extra, far_ref, got_ref, misc_ref, out_ref):
    half = CHUNK // 2
    own = far_ref[...]
    for i in range(2):
        rows = slice(i * half, (i + 1) * half)
        part = own[rows]
        if i == offset:
            part = part + got_ref[:half, :].astype(f32)
        out_ref[rows, :] = part.astype(bf16)
    extra = misc_ref[...]
    if with_extra:
        extra = extra + got_ref[half:, :]
    out_ref[CHUNK:, :] = extra


def step_kernel(near_ref, got_ref, misc_ref, out_ref):
    out_ref[:CHUNK, :] = (near_ref[...] + got_ref[:CHUNK, :].astype(f32)).astype(bf16)
    out_ref[CHUNK:, :] = misc_ref[...] + got_ref[CHUNK:, :]


def finish_kernel(near_ref, up_ref, down_ref, misc_ref, p_ref, grad_ref, center_ref, loss_ref):
    @pl.when(pl.program_id(0) == 0)
    def _():
        grad_ref[...] = near_ref[...] + up_ref[:CHUNK, :].astype(f32) + down_ref[:CHUNK, :].astype(f32)

    extra = (misc_ref[...] + up_ref[CHUNK:, :] + down_ref[CHUNK:, :]).astype(f32)
    first = extra[0:8] + extra[8:16] + extra[16:24]
    loss = extra[24:32] + extra[32:40] + extra[40:48]
    total = jnp.broadcast_to(jnp.sum(first, axis=0, keepdims=True), (16, D))
    loss_ref[...] = jnp.broadcast_to(jnp.sum(loss, axis=0, keepdims=True), (8, D))
    stacked = jnp.concatenate(split3(total), axis=0)
    three = dot(stacked, p_ref[...])
    center_ref[...] = (three[0:1] + three[16:17] + three[32:33]) * (1.0 / TOTAL)


def finish(near, up, down, misc, prototypes):
    width = prototypes.shape[1]
    block = 2048
    rows = CHUNK + EXTRA
    return pl.pallas_call(
        finish_kernel,
        grid=(width // block,),
        in_specs=[
            pl.BlockSpec((CHUNK, D), lambda i: (0, 0)),
            pl.BlockSpec((rows, D), lambda i: (0, 0)),
            pl.BlockSpec((rows, D), lambda i: (0, 0)),
            pl.BlockSpec((EXTRA, D), lambda i: (0, 0)),
            pl.BlockSpec((D, block), lambda i: (0, i)),
        ],
        out_specs=[
            pl.BlockSpec((CHUNK, D), lambda i: (0, 0)),
            pl.BlockSpec((1, block), lambda i: (0, i)),
            pl.BlockSpec((8, D), lambda i: (0, 0)),
        ],
        out_shape=[
            jax.ShapeDtypeStruct((CHUNK, D), f32),
            jax.ShapeDtypeStruct((1, width), f32),
            jax.ShapeDtypeStruct((8, D), f32),
        ],
        compiler_params=params(),
        cost_estimate=cost(6 * 8 * D * width, 5 << 20),
    )(near, up, down, misc, prototypes)


def final_kernel(count_ref, index_ref, s_ref, du_ref, out_ref):
    for i in range(LOCAL):
        pick = picks(index_ref, count_ref[i], i)
        unit, length = unit_rows(dot(pick, s_ref[i], TN))
        d_unit = du_ref[:, i * SLOTS : (i + 1) * SLOTS].astype(f32).T
        row = (d_unit - unit * jnp.sum(unit * d_unit, axis=1, keepdims=True)) / length
        top = row.astype(bf16)
        rest = (row - top.astype(f32)).astype(bf16)
        out_ref[i] = dot(pick, top) + dot(pick, rest)


def shards(student_rows, teacher_rows, prototypes, center, mask_index, mask_count, loss_scale):
    z, core, x, y = (lax.axis_index(a) for a in ("z", "core", "x", "y"))
    ids = jnp.concatenate([jnp.stack([z, core, x, y]).astype(jnp.int32), mask_count])
    down = [(i, (i - 1) % Z) for i in range(Z)]
    up = [(i, (i + 1) % Z) for i in range(Z)]

    mine = prep(mask_count, mask_index, student_rows, teacher_rows)
    other = swap(mine, "core", CORES, 1)
    stats, row_sum, turned, shifts = local_stats(ids, prototypes, center, mine, other)

    shape = jax.ShapeDtypeStruct((8, BOTH), f32)
    stats = small_call(core_merge_kernel, shape, stats, swap(stats, "core", CORES, 1))
    stats = small_call(merge_kernel, shape, stats, *[swap(stats, "y", Y, k) for k in (1, 2, 3)])
    coef, misc = small_call(
        last_merge_kernel,
        [shape, jax.ShapeDtypeStruct((EXTRA, D), bf16)],
        loss_scale.reshape(1),
        ids,
        stats,
        *[swap(stats, "x", X, k) for k in (1, 2, 3)],
        row_sum,
        smem=(0, 1),
    )

    common = (turned, shifts, prototypes, mine, other, coef, misc)
    step_shape = jax.ShapeDtypeStruct((CHUNK + EXTRA, D), bf16)
    half_a, half_b, du_a = grads(ids, [4], True, *common)
    from_up = lax.ppermute(half_a, "z", down)
    from_down = lax.ppermute(half_b, "z", up)
    far_down, far_up, du_b = grads(ids, [-3, 3], False, *common)
    send_down = small_call(functools.partial(halves_kernel, 0, True), step_shape, far_down, from_up, misc)
    send_up = small_call(functools.partial(halves_kernel, 1, False), step_shape, far_up, from_down, misc)
    from_up = lax.ppermute(send_down, "z", down)
    from_down = lax.ppermute(send_up, "z", up)
    *near, du_c = grads(ids, [-2, 2, -1, 1, 0], False, *common)
    for i in (0, 2):
        send_down = small_call(step_kernel, step_shape, near[i], from_up, misc)
        send_up = small_call(step_kernel, step_shape, near[i + 1], from_down, misc)
        from_up = lax.ppermute(send_down, "z", down)
        from_down = lax.ppermute(send_up, "z", up)
    proto_grad, patch_center, loss = finish(near[4], from_up, from_down, misc, prototypes)

    send = small_call(
        du_send_kernel, jax.ShapeDtypeStruct((CORES, D, ROWS), bf16), ids, du_a, du_b, du_c, smem=(0,)
    )
    part = D // (X * Y)
    got = lax.all_to_all(send.reshape(CORES * X * Y, part, ROWS), ("core", "x", "y"), 0, 0)
    own = small_call(du_sum_kernel, jax.ShapeDtypeStruct((X * Y, part, ROWS), bf16), got)
    du = lax.all_to_all(own, ("x", "y"), 0, 0).reshape(D, ROWS)
    student_grad = small_call(
        final_kernel,
        jax.ShapeDtypeStruct(student_rows.shape, f32),
        mask_count, mask_index, student_rows, du,
        smem=(0,),
    )
    return (loss[0, 0], student_grad, proto_grad, patch_center.reshape(-1))


def solution(mesh):
    fine = Mesh(mesh.devices.reshape(Z, CORES, X, Y), ("z", "core", "x", "y"))
    dp, proto = ("z", "core"), ("x", "y")
    in_specs = (
        P(dp, None, None),
        P(dp, None, None),
        P(None, proto),
        P(proto),
        P(dp, None),
        P(dp),
        P(),
    )
    out_specs = (P(), P(dp, None, None), P(proto + dp, None), P(proto))
    return jax.shard_map(shards, mesh=fine, in_specs=in_specs, out_specs=out_specs, check_vma=False)
```

time: 138 us -> 116 us (0.84); the launches traced: 135 us -> 116 us
  starting transfers between devices: 49.5 us -> 31.8 us
  blocking collectives: 0 us -> 14 us
  waiting for transfers between devices: 22.2 us -> 14.6 us
  Pallas kernels: 50.5 us -> 44.1 us
  other arithmetic: 5.71 us -> 0.01 us
  local copies, waits for them, and re-layouts: 5.4 us -> 9.76 us
    ppermute x24 -> x8, starting transfers between devices: 32.7 us -> 8.77 us  [swap(): return lax.ppermute(value, axis, swapped(axis, size, bit))]
    all_to_all x0 -> x1, blocking collectives: none -> 14 us  [shards(): du = lax.all_to_all(own, ('x', 'y'), 0, 0).reshape(D, ROWS)]
    pallas_call x6 -> x1, Pallas kernels: 12.6 us -> 2.45 us  [finish(): pl.pallas_call(finish_kernel, grid=(width // block,), in_specs=[pl.BlockS...]
    pallas_call x5 -> x12, Pallas kernels: 0.29 us -> 7.99 us  [small_call(): pl.pallas_call(kernel, out_shape=out_shape, in_specs=specs, out_specs=jax...]
    ppermute x4 -> x0, starting transfers between devices: 7.22 us -> none  [the longest x1 3.77 us: shards(): lax.ppermute((near[2] + from_up.astype(f32)).astype(bf16), 'z', down)]
    ppermute x1 -> x3, starting transfers between devices: 3.49 us -> 10.3 us  [shards(): from_up = lax.ppermute(send_down, 'z', down)]
    all_to_all x0 -> x1, starting transfers between devices: none -> 6.52 us  [shards(): lax.all_to_all(send.reshape(CORES * X * Y, part, ROWS), ('core', 'x', 'y'...]
    ppermute x24 -> x8, waiting for transfers between devices: 14.3 us -> 8.62 us  [swap(): return lax.ppermute(value, axis, swapped(axis, size, bit))]
  transfers between devices with their start and end apart: 32 -> 17, of which waited for: 13 -> 8; matrix products, arithmetic and copies ran while one was open for 3% -> 1% of each run, Pallas kernels for 24% -> 20%
where the time goes in v2:
time: 116 us
  Pallas kernels  44.1 us (38%)
  starting transfers between devices  31.8 us (27%)
  waiting for transfers between devices  14.6 us (13%)
  blocking collectives  14 us (12%)
  local copies, waits for them, and re-layouts  9.76 us (8%)
  between operations  1.52 us (1%)
    pallas_call x3, Pallas kernels, grads(): pl.pallas_call(functools.partial(grad_kernel, n, split), grid_spec=grid,...  18.8 us
    all_to_all x1, blocking collectives, shards(): du = lax.all_to_all(own, ('x', 'y'), 0, 0).reshape(D, ROWS)  14 us
    pallas_call x1, Pallas kernels, local_stats(): pl.pallas_call(stats_kernel, grid_spec=grid, out_shape=[jax.ShapeDtypeStr...  13.8 us
    ppermute x3, starting transfers between devices, shards(): from_up = lax.ppermute(send_down, 'z', down)  10.3 us
    ppermute x8, starting transfers between devices, swap(): return lax.ppermute(value, axis, swapped(axis, size, bit))  8.77 us
    ppermute x8, waiting for transfers between devices, swap(): return lax.ppermute(value, axis, swapped(axis, size, bit))  8.62 us
    unnamed x34, local copies, waits for them, and re-layouts  8.52 us
    pallas_call x12, Pallas kernels, small_call(): pl.pallas_call(kernel, out_shape=out_shape, in_specs=specs, out_specs=jax...  7.99 us
  transfers between devices with their start and end apart: 17, of which 8 were waited for; matrix products, arithmetic and copies ran while one was open for 1% of the time, Pallas kernels for 20%

profile of v2, /device:TPU:8, one launch (start us, length us, event | category | flops | bytes accessed | tf_op | source)
XLA Modules:
  0.0 115.8 jit_solution(8752170723973295477)
XLA Ops:
  0.6 0.0 copy-start.3
  0.6 1.0 copy-done.3
  1.7 1.0 copy-done.5
  2.7 0.7 copy-done.10
  3.4 0.7 copy-done.12
  4.1 1.1 shard_map.129.mine_ref
  5.1 0.1 collective-permute-start
  5.2 0.7 concatenate.3.ids_ref
  6.0 1.2 collective-permute-done.other_ref
  7.1 0.8 copy-done.14
  7.9 13.8 %shard_map.130 = (f32[8,1024]{1,0:T(8,128)S(1)}, f32[8,256]{1,0:T(8,128)S(1)}, bf16[8,512,256]{2,1,0:T(8,128)(2,1)S(1)}, f32[8,512,128]{2,1,0:T(8,128)S(1)}) custom-call(s32[8]{0:T(128)S(1)} %concatenate.3.ids_ref, bf16[256,8192]{1,0:T(8,128)(2,1)} %p_ref.9, f32[16,1,512]{2,1,0:T(1,128)S(1)} %bitcast.12, bf16[2,512,256]{2,1,0:T(8,128)(2,1)S(1)} %shard_map.129.mine_ref, ...), custom_call_target="tpu_custom_call" | custom-call | flops 4294967296 | bytes 6291456 | tf_op jit(solution)/shard_map/pallas_call | solution.py:160
  21.7 1.3 %copy-done.2 = f32[8,512,128]{2,1,0:T(8,128)} copy-done((f32[8,512,128]{2,1,0:T(8,128)}, f32[8,512,128]{2,1,0:T(8,128)S(1)}, u32[]{:S(2)}) %copy-start.2) | copy-done | bytes 2097176
  23.0 0.1 collective-permute-start.1
  23.2 1.1 collective-permute-done.1.got_ref
  24.3 1.7 %collective-permute-start.4 = (f32[8,1024]{1,0:T(8,128)S(1)}, f32[8,1024]{1,0:T(8,128)S(1)}, u32[]{:S(2)}, u32[]{:S(2)}) collective-permute-start(f32[8,1024]{1,0:T(8,128)S(1)} %shard_map.131.refs_0_), channel_id=1, source_target_pairs={{0,3},{1,2},{2,1},{3,0},{4,7},{5,6},{6,5},{7,4},{8,11},{9,10},{10,... | collective-permute-start | bytes 98312 | tf_op jit(solution)/shard_map/ppermute | solution.py:260
  26.0 2.7 %collective-permute-start.3 = (f32[8,1024]{1,0:T(8,128)S(1)}, f32[8,1024]{1,0:T(8,128)S(1)}, u32[]{:S(2)}, u32[]{:S(2)}) collective-permute-start(f32[8,1024]{1,0:T(8,128)S(1)} %shard_map.131.refs_0_), channel_id=1, source_target_pairs={{0,2},{1,3},{2,0},{3,1},{4,6},{5,7},{6,4},{7,5},{8,10},{9,11},{10,... | collective-permute-start | bytes 98312 | tf_op jit(solution)/shard_map/ppermute | solution.py:260
  28.6 0.0 collective-permute-start.2
  28.7 3.0 %collective-permute-done.3.refs_2_ = f32[8,1024]{1,0:T(8,128)S(1)} collective-permute-done((f32[8,1024]{1,0:T(8,128)S(1)}, f32[8,1024]{1,0:T(8,128)S(1)}, u32[]{:S(2)}, u32[]{:S(2)}) %collective-permute-start.3) | collective-permute-done | bytes 32800 | tf_op jit(solution)/shard_map/ppermute | solution.py:260
  31.6 0.9 collective-permute-done.2.refs_1_
  32.6 0.1 shard_map.132.a
  32.6 1.9 %collective-permute-start.7 = (f32[8,1024]{1,0:T(8,128)S(1)}, f32[8,1024]{1,0:T(8,128)S(1)}, u32[]{:S(2)}, u32[]{:S(2)}) collective-permute-start(f32[8,1024]{1,0:T(8,128)S(1)} %shard_map.132.a), channel_id=1, source_target_pairs={{0,12},{4,8},{8,4},{12,0},{1,13},{5,9},{9,5},{13,1},{2,14},{6,10},... | collective-permute-start | bytes 98312 | tf_op jit(solution)/shard_map/ppermute | solution.py:260
  34.5 0.8 collective-permute-start.6
  35.4 1.4 %collective-permute-start.5 = (f32[8,1024]{1,0:T(8,128)S(1)}, f32[8,1024]{1,0:T(8,128)S(1)}, u32[]{:S(2)}, u32[]{:S(2)}) collective-permute-start(f32[8,1024]{1,0:T(8,128)S(1)} %shard_map.132.a), channel_id=1, source_target_pairs={{0,4},{4,0},{8,12},{12,8},{1,5},{5,1},{9,13},{13,9},{2,6},{6,2},{1... | collective-permute-start | bytes 98312 | tf_op jit(solution)/shard_map/ppermute | solution.py:260
  37.5 0.4 collective-permute-done.7.d
  37.8 2.1 %collective-permute-done.6.c = f32[8,1024]{1,0:T(8,128)S(1)} collective-permute-done((f32[8,1024]{1,0:T(8,128)S(1)}, f32[8,1024]{1,0:T(8,128)S(1)}, u32[]{:S(2)}, u32[]{:S(2)}) %collective-permute-start.6) | collective-permute-done | bytes 32800 | tf_op jit(solution)/shard_map/ppermute | solution.py:260
  40.0 0.0 collective-permute-done.5.b
  40.0 0.7 shard_map.133
  40.7 3.2 %shard_map.136 = (bf16[304,256]{1,0:T(8,128)(2,1)S(1)}, bf16[256,256]{1,0:T(8,128)(2,1)S(1)}, f32[256,1024]{1,0:T(8,128)S(1)}) custom-call(s32[8]{0:T(128)S(1)} %concatenate.3.ids_ref, s32[1]{0:T(128)S(6)} %rem.62.order_ref, bf16[8,512,256]{2,1,0:T(8,128)(2,1)S(1)} %get-tuple-element.25.pt_ref, f32[8,512,128]{2,1,0:T(8,128)} %copy-done.2, ...), custom_call_target="tpu_custom_call" | custom-call | flops 1073741824 | bytes 3145728 | tf_op jit(solution)/shard_map/pallas_call | solution.py:324
  43.9 2.0 %collective-permute-start.12 = (bf16[256,256]{1,0:T(8,128)(2,1)S(1)}, bf16[256,256]{1,0:T(8,128)(2,1)S(1)}, u32[]{:S(2)}, u32[]{:S(2)}) collective-permute-start(bf16[256,256]{1,0:T(8,128)(2,1)S(1)} %get-tuple-element.39), channel_id=1, source_target_pairs={{0,32},{32,64},{64,96},{96,128},{128,160},{160,192},{192,224},{224... | collective-permute-start | bytes 393224 | tf_op jit(solution)/shard_map/ppermute | solution.py:448
  45.9 4.0 %collective-permute-start.8 = (bf16[304,256]{1,0:T(8,128)(2,1)S(1)}, bf16[304,256]{1,0:T(8,128)(2,1)S(1)}, u32[]{:S(2)}, u32[]{:S(2)}) collective-permute-start(bf16[304,256]{1,0:T(8,128)(2,1)S(1)} %get-tuple-element.35), channel_id=1, source_target_pairs={{0,224},{32,0},{64,32},{96,64},{128,96},{160,128},{192,160},{224,1... | collective-permute-start | bytes 466952 | tf_op jit(solution)/shard_map/ppermute | solution.py:447
  49.9 5.1 %shard_map.135 = (f32[512,256]{1,0:T(8,128)S(1)}, f32[512,256]{1,0:T(8,128)S(1)}, f32[256,1024]{1,0:T(8,128)S(1)}) custom-call(s32[8]{0:T(128)S(1)} %concatenate.3.ids_ref, s32[2]{0:T(128)S(1)} %compare_select_fusion.order_ref, bf16[8,512,256]{2,1,0:T(8,128)(2,1)S(1)} %get-tuple-element.25.pt_ref, f32[8,512,128]{2,1,0:T(8,128)} %copy-done.2, ...), custom_call_target="tpu_custom_call" | custom-call | flops 2147483648 | bytes 3145728 | tf_op jit(solution)/shard_map/pallas_call | solution.py:324
  55.0 0.0 collective-permute-done.12.got_ref
  55.0 0.8 shard_map.140
  55.8 0.0 collective-permute-start.13
  55.8 0.0 collective-permute-done.8.got_ref
  55.8 0.8 shard_map.137
  56.6 3.2 %collective-permute-start.9 = (bf16[560,256]{1,0:T(8,128)(2,1)}, bf16[560,256]{1,0:T(8,128)(2,1)}, u32[]{:S(2)}, u32[]{:S(2)}) collective-permute-start(bf16[560,256]{1,0:T(8,128)(2,1)} %shard_map.137), channel_id=1, source_target_pairs={{0,224},{32,0},{64,32},{96,64},{128,96},{160,128},{192,160},{224,1... | collective-permute-start | bytes 860168 | tf_op jit(solution)/shard_map/ppermute | solution.py:452
  59.8 10.5 %shard_map.134 = (f32[512,256]{1,0:T(8,128)S(1)}, f32[512,256]{1,0:T(8,128)S(1)}, f32[512,256]{1,0:T(8,128)S(1)}, f32[512,256]{1,0:T(8,128)S(1)}, f32[512,256]{1,0:T(8,128)S(1)}, /*index=5*/f32[256,1024]{1,0:T(8,128)S(1)}) custom-call(s32[8]{0:T(128)S(1)} %concatenate.3.ids_ref, s32[5]{0:T(128)S(1)} %compare_select_fusion.2.order_ref, ...), custom_call_target="tpu_custom_call" | custom-call | flops 5368709120 | bytes 3145728 | tf_op jit(solution)/shard_map/pallas_call | solution.py:324
  70.3 0.0 copy-start.6
  70.3 0.8 copy-done.6
  71.1 1.5 %shard_map.144 = bf16[2,256,512]{2,1,0:T(8,128)(2,1)} custom-call(s32[8]{0:T(128)S(1)} %concatenate.3.ids_ref, f32[256,1024]{1,0:T(8,128)S(1)} %get-tuple-element.41.a, f32[256,1024]{1,0:T(8,128)S(1)} %get-tuple-element.42.b, f32[256,1024]{1,0:T(8,128)S(1)} %get-tuple-element.43.c), custom_call_target="tpu_custom_call" | custom-call | flops 1048576 | bytes 262144 | tf_op jit(solution)/shard_map/pallas_call | solution.py:245
  72.6 6.5 %all-to-all-start = ((bf16[32,16,512]{2,1,0:T(8,128)(2,1)}), bf16[32,16,512]{2,1,0:T(8,128)(2,1)S(1)}, u32[]{:S(2)}, u32[]{:S(2)}) async-start(bf16[32,16,512]{2,1,0:T(8,128)(2,1)} %bitcast.7), calls=%async_computation | async-start | bytes 1048576 | tf_op jit(solution)/shard_map/all_to_all | solution.py:466
  79.1 0.1 shard_map.141
  79.2 0.1 collective-permute-start.14
  79.3 0.0 collective-permute-done.9.got_ref
  79.3 0.0 copy-start.4
  79.3 0.0 copy-start.11
  79.3 0.0 copy-start.13
  79.4 1.1 shard_map.138
  80.4 3.3 %collective-permute-start.10 = (bf16[560,256]{1,0:T(8,128)(2,1)S(1)}, bf16[560,256]{1,0:T(8,128)(2,1)S(1)}, u32[]{:S(2)}, u32[]{:S(2)}) collective-permute-start(bf16[560,256]{1,0:T(8,128)(2,1)S(1)} %shard_map.138), channel_id=1, source_target_pairs={{0,224},{32,0},{64,32},{96,64},{128,96},{160,128},{192,160},{224,1... | collective-permute-start | bytes 860168 | tf_op jit(solution)/shard_map/ppermute | solution.py:458
  83.7 5.7 %collective-permute-done.14.got_ref = bf16[560,256]{1,0:T(8,128)(2,1)S(1)} collective-permute-done((bf16[560,256]{1,0:T(8,128)(2,1)S(1)}, bf16[560,256]{1,0:T(8,128)(2,1)S(1)}, u32[]{:S(2)}, u32[]{:S(2)}) %collective-permute-start.14) | collective-permute-done | bytes 286752 | tf_op jit(solution)/shard_map/ppermute | solution.py:459
  89.4 0.1 shard_map.142
  89.5 0.1 collective-permute-start.15
  89.5 0.3 collective-permute-done.10.got_ref
  89.8 0.1 shard_map.139
  89.9 3.8 %collective-permute-start.11 = (bf16[560,256]{1,0:T(8,128)(2,1)S(1)}, bf16[560,256]{1,0:T(8,128)(2,1)S(1)}, u32[]{:S(2)}, u32[]{:S(2)}) collective-permute-start(bf16[560,256]{1,0:T(8,128)(2,1)S(1)} %shard_map.139), channel_id=1, source_target_pairs={{0,224},{32,0},{64,32},{96,64},{128,96},{160,128},{192,160},{224,1... | collective-permute-start | bytes 860168 | tf_op jit(solution)/shard_map/ppermute | solution.py:458
  93.7 0.0 all-to-all-done.got_ref
  93.7 0.1 shard_map.145
  93.8 14.0 %all_to_all.10 = bf16[16,16,512]{2,1,0:T(8,128)(2,1)S(1)} all-to-all(bf16[16,16,512]{2,1,0:T(8,128)(2,1)S(1)} %shard_map.145), channel_id=1, replica_groups=mesh['z'=8,'core'=2,'x'=4,'y'=4] {'x','y'}, dimensions={0} | all-to-all | bytes 524288 | tf_op jit(solution)/shard_map/all_to_all | solution.py:468
  107.8 2.9 %shard_map.146 = f32[4,256,256]{2,1,0:T(8,128)} custom-call(s32[4]{0:T(128)S(1)} %copy-done.13, s32[4,128]{1,0:T(4,128)S(1)} %copy-done.11, bf16[4,256,256]{2,1,0:T(8,128)(2,1)S(1)} %copy-done.4, bf16[256,512]{1,0:T(8,128)(2,1)S(1)} %bitcast.11), custom_call_target="tpu_custom_call" | custom-call | flops 1048576 | bytes 262144 | tf_op jit(solution)/shard_map/pallas_call | solution.py:245
  110.7 0.0 copy-start
  110.7 2.2 %copy-done = bf16[256,8192]{1,0:T(8,128)(2,1)S(1)} copy-done((bf16[256,8192]{1,0:T(8,128)(2,1)S(1)}, bf16[256,8192]{1,0:T(8,128)(2,1)}, u32[]{:S(2)}) %copy-start) | copy-done | bytes 4194328
  112.8 2.4 %shard_map.143 = (f32[512,256]{1,0:T(8,128)}, f32[1,8192]{1,0:T(1,128)}, f32[8,256]{1,0:T(8,128)S(1)}) custom-call(f32[512,256]{1,0:T(8,128)S(1)} %copy-done.9, bf16[560,256]{1,0:T(8,128)(2,1)S(1)} %collective-permute-done.11.up_ref, bf16[560,256]{1,0:T(8,128)(2,1)S(1)} %collective-permute-done.15.down_ref, bf16[48,256]{1,0:T(8,128)(2,1)S(1)} %get-tuple-element.30.misc_ref, ...), custom_call_target="tpu_custom_call" | custom-call | flops 100663296 | bytes 5242880 | tf_op jit(solution)/shard_map/pallas_call | solution.py:384
  115.3 0.5 slice.3
  (27 shorter events, 0.1 us)
Async XLA Ops:
  0.6 1.0 copy-start.3
  1.7 1.0 copy-start.5
  2.7 0.7 copy-start.10
  3.4 0.7 copy-start.12
  5.1 2.0 %collective-permute-start = (bf16[2,512,256]{2,1,0:T(8,128)(2,1)S(1)}, bf16[2,512,256]{2,1,0:T(8,128)(2,1)S(1)}, u32[]{:S(2)}, u32[]{:S(2)}) collective-permute-start(bf16[2,512,256]{2,1,0:T(8,128)(2,1)S(1)} %shard_map.129.mine_ref), channel_id=1, source_target_pairs={{0,16},{16,0},{1,17},{17,1},{2,18},{18,2},{3,19},{19,3},{4,20},{20... | collective-permute-start | bytes 1572872 | tf_op jit(solution)/shard_map/ppermute | solution.py:260
  7.1 0.8 copy-start.14
  7.9 20.8 %copy-start.16 = (s32[2]{0:T(128)S(1)}, s32[2]{0:T(128)}, u32[]{:S(2)}) copy-start(s32[2]{0:T(128)} %constant.41.clone) | copy-start | bytes 28
  7.9 28.9 %copy-start.15 = (s32[5]{0:T(128)S(1)}, s32[5]{0:T(128)}, u32[]{:S(2)}) copy-start(s32[5]{0:T(128)} %constant.42.clone) | copy-start | bytes 64
  21.7 1.3 %copy-start.2 = (f32[8,512,128]{2,1,0:T(8,128)}, f32[8,512,128]{2,1,0:T(8,128)S(1)}, u32[]{:S(2)}) copy-start(f32[8,512,128]{2,1,0:T(8,128)S(1)} %get-tuple-element.26.cb_ref) | copy-start | bytes 6291460
  23.0 26.8 %copy-start.1 = (bf16[8,512,256]{2,1,0:T(8,128)(2,1)}, bf16[8,512,256]{2,1,0:T(8,128)(2,1)S(1)}, u32[]{:S(2)}) copy-start(bf16[8,512,256]{2,1,0:T(8,128)(2,1)S(1)} %get-tuple-element.25.pt_ref) | copy-start | bytes 6291460
  23.0 1.2 %collective-permute-start.1 = (f32[8,1024]{1,0:T(8,128)S(1)}, f32[8,1024]{1,0:T(8,128)S(1)}, u32[]{:S(2)}, u32[]{:S(2)}) collective-permute-start(f32[8,1024]{1,0:T(8,128)S(1)} %get-tuple-element.27.mine_ref), channel_id=1, source_target_pairs={{0,16},{16,0},{1,17},{17,1},{2,18},{18,2},{3,19},{19,3},{4,20},{20... | collective-permute-start | bytes 98312 | tf_op jit(solution)/shard_map/ppermute | solution.py:260
  24.3 4.4 %collective-permute-start.4 = (f32[8,1024]{1,0:T(8,128)S(1)}, f32[8,1024]{1,0:T(8,128)S(1)}, u32[]{:S(2)}, u32[]{:S(2)}) collective-permute-start(f32[8,1024]{1,0:T(8,128)S(1)} %shard_map.131.refs_0_), channel_id=1, source_target_pairs={{0,3},{1,2},{2,1},{3,0},{4,7},{5,6},{6,5},{7,4},{8,11},{9,10},{10,... | collective-permute-start | bytes 98312 | tf_op jit(solution)/shard_map/ppermute | solution.py:260
  26.0 5.7 %collective-permute-start.3 = (f32[8,1024]{1,0:T(8,128)S(1)}, f32[8,1024]{1,0:T(8,128)S(1)}, u32[]{:S(2)}, u32[]{:S(2)}) collective-permute-start(f32[8,1024]{1,0:T(8,128)S(1)} %shard_map.131.refs_0_), channel_id=1, source_target_pairs={{0,2},{1,3},{2,0},{3,1},{4,6},{5,7},{6,4},{7,5},{8,10},{9,11},{10,... | collective-permute-start | bytes 98312 | tf_op jit(solution)/shard_map/ppermute | solution.py:260
  28.6 3.9 %collective-permute-start.2 = (f32[8,1024]{1,0:T(8,128)S(1)}, f32[8,1024]{1,0:T(8,128)S(1)}, u32[]{:S(2)}, u32[]{:S(2)}) collective-permute-start(f32[8,1024]{1,0:T(8,128)S(1)} %shard_map.131.refs_0_), channel_id=1, source_target_pairs={{0,1},{1,0},{2,3},{3,2},{4,5},{5,4},{6,7},{7,6},{8,9},{9,8},{10,11... | collective-permute-start | bytes 98312 | tf_op jit(solution)/shard_map/ppermute | solution.py:260
  32.6 5.2 %collective-permute-start.7 = (f32[8,1024]{1,0:T(8,128)S(1)}, f32[8,1024]{1,0:T(8,128)S(1)}, u32[]{:S(2)}, u32[]{:S(2)}) collective-permute-start(f32[8,1024]{1,0:T(8,128)S(1)} %shard_map.132.a), channel_id=1, source_target_pairs={{0,12},{4,8},{8,4},{12,0},{1,13},{5,9},{9,5},{13,1},{2,14},{6,10},... | collective-permute-start | bytes 98312 | tf_op jit(solution)/shard_map/ppermute | solution.py:260
  34.5 5.4 %collective-permute-start.6 = (f32[8,1024]{1,0:T(8,128)S(1)}, f32[8,1024]{1,0:T(8,128)S(1)}, u32[]{:S(2)}, u32[]{:S(2)}) collective-permute-start(f32[8,1024]{1,0:T(8,128)S(1)} %shard_map.132.a), channel_id=1, source_target_pairs={{0,8},{4,12},{8,0},{12,4},{1,9},{5,13},{9,1},{13,5},{2,10},{6,14},... | collective-permute-start | bytes 98312 | tf_op jit(solution)/shard_map/ppermute | solution.py:260
  35.4 4.6 %collective-permute-start.5 = (f32[8,1024]{1,0:T(8,128)S(1)}, f32[8,1024]{1,0:T(8,128)S(1)}, u32[]{:S(2)}, u32[]{:S(2)}) collective-permute-start(f32[8,1024]{1,0:T(8,128)S(1)} %shard_map.132.a), channel_id=1, source_target_pairs={{0,4},{4,0},{8,12},{12,8},{1,5},{5,1},{9,13},{13,9},{2,6},{6,2},{1... | collective-permute-start | bytes 98312 | tf_op jit(solution)/shard_map/ppermute | solution.py:260
  43.9 11.2 %collective-permute-start.12 = (bf16[256,256]{1,0:T(8,128)(2,1)S(1)}, bf16[256,256]{1,0:T(8,128)(2,1)S(1)}, u32[]{:S(2)}, u32[]{:S(2)}) collective-permute-start(bf16[256,256]{1,0:T(8,128)(2,1)S(1)} %get-tuple-element.39), channel_id=1, source_target_pairs={{0,32},{32,64},{64,96},{96,128},{128,160},{160,192},{192,224},{224... | collective-permute-start | bytes 393224 | tf_op jit(solution)/shard_map/ppermute | solution.py:448
  45.9 9.9 %collective-permute-start.8 = (bf16[304,256]{1,0:T(8,128)(2,1)S(1)}, bf16[304,256]{1,0:T(8,128)(2,1)S(1)}, u32[]{:S(2)}, u32[]{:S(2)}) collective-permute-start(bf16[304,256]{1,0:T(8,128)(2,1)S(1)} %get-tuple-element.35), channel_id=1, source_target_pairs={{0,224},{32,0},{64,32},{96,64},{128,96},{160,128},{192,160},{224,1... | collective-permute-start | bytes 466952 | tf_op jit(solution)/shard_map/ppermute | solution.py:447
  55.8 23.4 %collective-permute-start.13 = (bf16[560,256]{1,0:T(8,128)(2,1)}, bf16[560,256]{1,0:T(8,128)(2,1)S(1)}, u32[]{:S(2)}, u32[]{:S(2)}) collective-permute-start(bf16[560,256]{1,0:T(8,128)(2,1)} %shard_map.140), channel_id=1, source_target_pairs={{0,32},{32,64},{64,96},{96,128},{128,160},{160,192},{192,224},{224... | collective-permute-start | bytes 860168 | tf_op jit(solution)/shard_map/ppermute | solution.py:453
  56.6 22.7 %collective-permute-start.9 = (bf16[560,256]{1,0:T(8,128)(2,1)}, bf16[560,256]{1,0:T(8,128)(2,1)}, u32[]{:S(2)}, u32[]{:S(2)}) collective-permute-start(bf16[560,256]{1,0:T(8,128)(2,1)} %shard_map.137), channel_id=1, source_target_pairs={{0,224},{32,0},{64,32},{96,64},{128,96},{160,128},{192,160},{224,1... | collective-permute-start | bytes 860168 | tf_op jit(solution)/shard_map/ppermute | solution.py:452
  70.3 0.8 copy-start.6
  71.1 1.5 %copy-start.8 = (f32[512,256]{1,0:T(8,128)}, f32[512,256]{1,0:T(8,128)S(1)}, u32[]{:S(2)}) copy-start(f32[512,256]{1,0:T(8,128)S(1)} %get-tuple-element.31.near_ref) | copy-start | bytes 1572868
  71.1 8.2 %copy-start.7 = (f32[512,256]{1,0:T(8,128)S(1)}, f32[512,256]{1,0:T(8,128)}, u32[]{:S(2)}) copy-start(f32[512,256]{1,0:T(8,128)} %copy-done.6) | copy-start | bytes 1572868
  72.6 21.1 %all-to-all-start = ((bf16[32,16,512]{2,1,0:T(8,128)(2,1)}), bf16[32,16,512]{2,1,0:T(8,128)(2,1)S(1)}, u32[]{:S(2)}, u32[]{:S(2)}) async-start(bf16[32,16,512]{2,1,0:T(8,128)(2,1)} %bitcast.7), calls=%async_computation | async-start | bytes 1048576 | tf_op jit(solution)/shard_map/all_to_all | solution.py:466
  79.2 10.2 %collective-permute-start.14 = (bf16[560,256]{1,0:T(8,128)(2,1)S(1)}, bf16[560,256]{1,0:T(8,128)(2,1)S(1)}, u32[]{:S(2)}, u32[]{:S(2)}) collective-permute-start(bf16[560,256]{1,0:T(8,128)(2,1)S(1)} %shard_map.141), channel_id=1, source_target_pairs={{0,32},{32,64},{64,96},{96,128},{128,160},{160,192},{192,224},{224... | collective-permute-start | bytes 860168 | tf_op jit(solution)/shard_map/ppermute | solution.py:459
  79.3 28.5 %copy-start.4 = (bf16[4,256,256]{2,1,0:T(8,128)(2,1)S(1)}, bf16[4,256,256]{2,1,0:T(8,128)(2,1)}, u32[]{:S(2)}) copy-start(bf16[4,256,256]{2,1,0:T(8,128)(2,1)} %s_ref.3) | copy-start | bytes 1572868
  79.3 28.4 %copy-start.11 = (s32[4,128]{1,0:T(4,128)S(1)}, s32[4,128]{1,0:T(4,128)}, u32[]{:S(2)}) copy-start(s32[4,128]{1,0:T(4,128)} %index_ref.3) | copy-start | bytes 6148
  79.3 28.4 %copy-start.13 = (s32[4]{0:T(128)S(1)}, s32[4]{0:T(128)}, u32[]{:S(2)}) copy-start(s32[4]{0:T(128)} %count_ref.3) | copy-start | bytes 52
  80.4 9.4 %collective-permute-start.10 = (bf16[560,256]{1,0:T(8,128)(2,1)S(1)}, bf16[560,256]{1,0:T(8,128)(2,1)S(1)}, u32[]{:S(2)}, u32[]{:S(2)}) collective-permute-start(bf16[560,256]{1,0:T(8,128)(2,1)S(1)} %shard_map.138), channel_id=1, source_target_pairs={{0,224},{32,0},{64,32},{96,64},{128,96},{160,128},{192,160},{224,1... | collective-permute-start | bytes 860168 | tf_op jit(solution)/shard_map/ppermute | solution.py:458
  89.5 21.2 %collective-permute-start.15 = (bf16[560,256]{1,0:T(8,128)(2,1)S(1)}, bf16[560,256]{1,0:T(8,128)(2,1)S(1)}, u32[]{:S(2)}, u32[]{:S(2)}) collective-permute-start(bf16[560,256]{1,0:T(8,128)(2,1)S(1)} %shard_map.142), channel_id=1, source_target_pairs={{0,32},{32,64},{64,96},{96,128},{128,160},{160,192},{192,224},{224... | collective-permute-start | bytes 860168 | tf_op jit(solution)/shard_map/ppermute | solution.py:459
  89.8 20.8 %copy-start.9 = (f32[512,256]{1,0:T(8,128)S(1)}, f32[512,256]{1,0:T(8,128)}, u32[]{:S(2)}) copy-start(f32[512,256]{1,0:T(8,128)} %copy-done.8) | copy-start | bytes 1572868
  89.9 20.8 %collective-permute-start.11 = (bf16[560,256]{1,0:T(8,128)(2,1)S(1)}, bf16[560,256]{1,0:T(8,128)(2,1)S(1)}, u32[]{:S(2)}, u32[]{:S(2)}) collective-permute-start(bf16[560,256]{1,0:T(8,128)(2,1)S(1)} %shard_map.139), channel_id=1, source_target_pairs={{0,224},{32,0},{64,32},{96,64},{128,96},{160,128},{192,160},{224,1... | collective-permute-start | bytes 860168 | tf_op jit(solution)/shard_map/ppermute | solution.py:458
  110.7 2.2 %copy-start = (bf16[256,8192]{1,0:T(8,128)(2,1)S(1)}, bf16[256,8192]{1,0:T(8,128)(2,1)}, u32[]{:S(2)}) copy-start(bf16[256,8192]{1,0:T(8,128)(2,1)} %p_ref.9) | copy-start | bytes 12582916

commit v3 on v2

v3 whole, which is shorter than its diff:
```python
import functools
import math

import jax
import jax.numpy as jnp
from jax import lax
from jax.experimental import pallas as pl
from jax.experimental.pallas import tpu as pltpu
from jax.sharding import Mesh, PartitionSpec as P

bf16 = jnp.bfloat16
f32 = jnp.float32
log2e = math.log2(math.e)
ln2 = math.log(2.0)
t_scale = log2e / 0.04
s_scale = log2e / 0.1
inverse_temp = 10.0
norm_epsilon = 1e-06
low = -1e30

Z, CORES, X, Y = 8, 2, 4, 4
D = 256
SLOTS = 128
IMAGES = 64
TOTAL = 4096
LOCAL = 4
ROWS = LOCAL * SLOTS
BOTH = 2 * ROWS
CHUNK = 512
TILE = 512
STAT_TILE = 256
EXTRA = 48
HELD = ROWS + 16
STATS = 5
PEERS = CORES * X * Y

NT = (((1,), (1,)), ((), ()))
TN = (((0,), (0,)), ((), ()))


def dot(a, b, dims=(((1,), (0,)), ((), ()))):
    return lax.dot_general(a, b, dims, preferred_element_type=f32)


def params():
    return pltpu.CompilerParams(vmem_limit_bytes=32 * 1024 * 1024)


def cost(flops, nbytes, trans=0):
    return pl.CostEstimate(flops=flops, bytes_accessed=nbytes, transcendentals=trans)


def picks(index_ref, count, i):
    patch = lax.broadcasted_iota(jnp.int32, (D, SLOTS), 0)
    slot = lax.broadcasted_iota(jnp.int32, (D, SLOTS), 1)
    hit = (patch == index_ref[i : i + 1, :]) & (slot < count)
    return jnp.where(hit, 1.0, 0.0).astype(bf16)


def unit_rows(values):
    length = jnp.sqrt(jnp.sum(values * values, axis=1, keepdims=True) + norm_epsilon)
    return values / length, length


def prep_kernel(count_ref, index_ref, s_ref, t_ref, out_ref):
    for i in range(LOCAL):
        pick = picks(index_ref, count_ref[i], i)
        for which, ref in enumerate((s_ref, t_ref)):
            unit, _ = unit_rows(dot(pick, ref[i], TN))
            out_ref[which, i * SLOTS : (i + 1) * SLOTS, :] = unit.astype(bf16)
    row = lax.broadcasted_iota(jnp.int32, (HELD - ROWS, D), 0)
    counts = jnp.zeros((HELD - ROWS, D), jnp.int32)
    for i in range(LOCAL):
        counts = jnp.where(row == i, count_ref[i], counts)
    for which in range(2):
        out_ref[which, ROWS:, :] = counts.astype(f32).astype(bf16)


def prep(count, index, student, teacher):
    smem = pl.BlockSpec(memory_space=pltpu.SMEM)
    vmem = pl.BlockSpec(memory_space=pltpu.VMEM)
    return pl.pallas_call(
        prep_kernel,
        out_shape=jax.ShapeDtypeStruct((2, HELD, D), bf16),
        in_specs=[smem, vmem, vmem, vmem],
        out_specs=vmem,
        compiler_params=params(),
        cost_estimate=cost(2 * 2 * ROWS * D * D, 1 << 21),
    )(count, index, student, teacher)


def wide(block, times):
    return jnp.concatenate([block] * times, axis=1)


def chunk_columns(i, core):
    return pl.ds(pl.multiple_of((CORES * i + core) * CHUNK, CHUNK), CHUNK)


def stats_kernel(ids_ref, p_ref, c_ref, mine_ref, other_ref, send_ref, sum_ref, pt_ref, cb_ref, acc, block):
    core = ids_ref[1]
    groups = (CHUNK // 8, 8, STAT_TILE)
    for i in range(Z):
        columns = chunk_columns(i, core)
        protos = p_ref[:, columns].T
        pt_ref[i] = protos
        column = jnp.broadcast_to(c_ref[:, columns] * -t_scale, (128, CHUNK)).T
        cb_ref[i] = column
        shift = wide(column, STAT_TILE // 128)
        for half, ref in enumerate((mine_ref, other_ref)):
            for j in range(ROWS // STAT_TILE):
                rows = slice(j * STAT_TILE, (j + 1) * STAT_TILE)
                at = slice(half * ROWS + j * STAT_TILE, half * ROWS + (j + 1) * STAT_TILE)
                t_arg = (dot(protos, ref[1, rows, :], NT) * t_scale + shift).reshape(groups)
                s_arg = (dot(protos, ref[0, rows, :], NT) * s_scale).reshape(groups)
                t_top = jnp.max(t_arg, axis=0)
                s_top = jnp.max(s_arg, axis=0)
                t_exp = jnp.exp2(t_arg - t_top[None])
                s_exp = jnp.exp2(s_arg - s_top[None])
                acc[0, i, :, at] = t_top
                acc[1, i, :, at] = jnp.sum(t_exp, axis=0)
                acc[2, i, :, at] = jnp.sum(t_exp * s_arg, axis=0)
                acc[3, i, :, at] = s_top
                acc[4, i, :, at] = jnp.sum(s_exp, axis=0)
    for g in range(BOTH // 128):
        at = slice(g * 128, (g + 1) * 128)
        parts = [acc[q, :, :, at].reshape(Z * 8, 128) for q in range(STATS)]
        t_top = jnp.max(parts[0], axis=0, keepdims=True)
        s_top = jnp.max(parts[3], axis=0, keepdims=True)
        t_keep = jnp.exp2(parts[0] - t_top)
        s_keep = jnp.exp2(parts[3] - s_top)
        merged_rows = (
            t_top,
            jnp.sum(parts[1] * t_keep, axis=0, keepdims=True),
            jnp.sum(parts[2] * t_keep, axis=0, keepdims=True),
            s_top,
            jnp.sum(parts[4] * s_keep, axis=0, keepdims=True),
        )
        for q in range(STATS):
            block[q * 8 + g : q * 8 + g + 1, :] = merged_rows[q]
    whole = block[...]
    for peer in range(PEERS):
        send_ref[peer] = whole
    first = jnp.sum(mine_ref[1, :ROWS, :].astype(f32), axis=0, keepdims=True)
    second = jnp.sum(other_ref[1, :ROWS, :].astype(f32), axis=0, keepdims=True)
    sum_ref[...] = jnp.broadcast_to(first + second, (8, D))


def local_stats(ids, prototypes, center, mine, other):
    smem = pl.BlockSpec(memory_space=pltpu.SMEM)
    vmem = pl.BlockSpec(memory_space=pltpu.VMEM)
    return pl.pallas_call(
        stats_kernel,
        in_specs=[smem, vmem, vmem, vmem, vmem],
        out_specs=[vmem] * 4,
        out_shape=[
            jax.ShapeDtypeStruct((PEERS, STATS * 8, 128), f32),
            jax.ShapeDtypeStruct((8, D), f32),
            jax.ShapeDtypeStruct((Z, CHUNK, D), bf16),
            jax.ShapeDtypeStruct((Z, CHUNK, 128), f32),
        ],
        scratch_shapes=[pltpu.VMEM((STATS, Z, 8, BOTH), f32), pltpu.VMEM((STATS * 8, 128), f32)],
        compiler_params=params(),
        cost_estimate=cost(4 * BOTH * Z * CHUNK * D, 6 << 20, 2 * BOTH * Z * CHUNK),
    )(ids, prototypes, center.reshape(1, -1), mine, other)


def split3(value):
    top = value.astype(bf16)
    rest = value - top.astype(f32)
    middle = rest.astype(bf16)
    return top, middle, (rest - middle.astype(f32)).astype(bf16)


def merge(parts):
    t_top = functools.reduce(jnp.maximum, [p[0] for p in parts])
    s_top = functools.reduce(jnp.maximum, [p[3] for p in parts])
    t_sum = cross = s_sum = 0.0
    for p in parts:
        t_keep = jnp.exp2(p[0] - t_top)
        t_sum = t_sum + p[1] * t_keep
        cross = cross + p[2] * t_keep
        s_sum = s_sum + p[4] * jnp.exp2(p[3] - s_top)
    return t_top, t_sum, cross, s_top, s_sum


def flip(value):
    return jnp.concatenate([value[LOCAL:], value[:LOCAL]], axis=0)


def merge_kernel(ids_ref, scale_ref, got_ref, mine_ref, other_ref, sum_ref, coef_ref, misc_ref):
    halves = []
    for core in range(CORES):
        parts = []
        for peer in range(core * X * Y, (core + 1) * X * Y):
            parts.append([got_ref[peer, q * 8 : (q + 1) * 8, :] for q in range(STATS)])
        halves.append(merge(parts))
    halves[1] = [flip(value) for value in halves[1]]
    here = ids_ref[1] == 0
    t_top, t_sum, cross, s_top, s_sum = [jnp.where(here, v, flip(v)) for v in merge(halves)]
    counts = [ref[0, ROWS:, :128].astype(f32)[:LOCAL] for ref in (mine_ref, other_ref)]
    count = jnp.concatenate(counts, axis=0)
    slot = lax.broadcasted_iota(jnp.int32, (8, 128), 1).astype(f32)
    live = slot < count
    weight = 1.0 / (IMAGES * jnp.maximum(count, 1.0))
    s_lse = s_top + jnp.log2(s_sum)
    ce = (s_lse - cross / t_sum) * ln2
    factor = jnp.log2(weight * (scale_ref[0] * inverse_temp))
    s_coef = jnp.where(live, factor - s_lse, low)
    t_coef = jnp.where(live, factor - t_top - jnp.log2(t_sum), low)
    for g in range(8):
        coef_ref[0:1, g * 128 : (g + 1) * 128] = s_coef[g : g + 1]
        coef_ref[1:2, g * 128 : (g + 1) * 128] = t_coef[g : g + 1]
    coef_ref[2:8, :] = jnp.zeros((6, BOTH), f32)
    part = jnp.sum(jnp.where(live, weight * ce, 0.0), axis=1, keepdims=True)
    first = jnp.sum(part[:LOCAL], axis=0, keepdims=True)
    second = jnp.sum(part[LOCAL:], axis=0, keepdims=True)
    row = lax.broadcasted_iota(jnp.int32, (EXTRA, D), 0)
    mine = jnp.bitwise_and(row, Z - 1) == ids_ref[0]
    row_sum = split3(sum_ref[0:1, :])
    losses = split3(jnp.broadcast_to(first + second, (1, D)))
    block = jnp.zeros((EXTRA, D), f32)
    for i in range(3):
        block = jnp.where(row // Z == i, row_sum[i].astype(f32), block)
        block = jnp.where(row // Z == 3 + i, losses[i].astype(f32), block)
    misc_ref[...] = jnp.where(mine, block, 0.0).astype(bf16)


def small_call(kernel, out_shape, *args, smem=()):
    specs = [
        pl.BlockSpec(memory_space=pltpu.SMEM if i in smem else pltpu.VMEM) for i in range(len(args))
    ]
    vmem = pl.BlockSpec(memory_space=pltpu.VMEM)
    return pl.pallas_call(
        kernel,
        out_shape=out_shape,
        in_specs=specs,
        out_specs=jax.tree.map(lambda _: vmem, out_shape),
        compiler_params=params(),
        cost_estimate=cost(1 << 20, 1 << 18),
    )(*args)


def grad_kernel(ids_ref, pt_ref, cb_ref, p_ref, mine_ref, other_ref, coef_ref, misc_ref, out_ref, send_ref, du_ref):
    core = ids_ref[1]
    for i in range(Z):
        protos = pt_ref[i]
        shift = wide(cb_ref[i], TILE // 128)
        wide_p = p_ref[:, chunk_columns(i, core)]
        total = None
        for half, ref in enumerate((mine_ref, other_ref)):
            for j in range(ROWS // TILE):
                rows = slice(j * TILE, (j + 1) * TILE)
                at = slice(half * ROWS + j * TILE, half * ROWS + (j + 1) * TILE)
                s_rows = ref[0, rows, :]
                t_arg = dot(protos, ref[1, rows, :], NT) * t_scale + shift + coef_ref[1:2, at]
                s_arg = dot(protos, s_rows, NT) * s_scale + coef_ref[0:1, at]
                dlogit = (jnp.exp2(s_arg) - jnp.exp2(t_arg)).astype(bf16)
                part = dot(dlogit, s_rows)
                total = part if total is None else total + part
                du = dot(wide_p, dlogit)
                if i == 0:
                    du_ref[:, at] = du
                else:
                    du_ref[:, at] += du
        out_ref[i, :CHUNK, :] = total.astype(bf16)
        out_ref[i, CHUNK:, :] = misc_ref[...]
    send_ref[core] = du_ref[:, :ROWS].astype(bf16)
    send_ref[1 - core] = du_ref[:, ROWS:].astype(bf16)


def grads(ids, turned, shifts, prototypes, mine, other, coef, misc):
    smem = pl.BlockSpec(memory_space=pltpu.SMEM)
    vmem = pl.BlockSpec(memory_space=pltpu.VMEM)
    return pl.pallas_call(
        grad_kernel,
        in_specs=[smem] + [vmem] * 7,
        out_specs=[vmem] * 2,
        out_shape=[
            jax.ShapeDtypeStruct((Z, CHUNK + EXTRA, D), bf16),
            jax.ShapeDtypeStruct((CORES, D, ROWS), bf16),
        ],
        scratch_shapes=[pltpu.VMEM((D, BOTH), f32)],
        compiler_params=params(),
        cost_estimate=cost(8 * BOTH * Z * CHUNK * D, 8 << 20, 2 * BOTH * Z * CHUNK),
    )(ids, turned, shifts, prototypes, mine, other, coef, misc)


def du_sum_kernel(got_ref, out_ref):
    total = jnp.sum(got_ref[...].astype(f32), axis=0).astype(bf16)
    out_ref[...] = jnp.broadcast_to(total[None], (X * Y,) + total.shape)


def finish_kernel(sum_ref, p_ref, grad_ref, center_ref, loss_ref):
    @pl.when(pl.program_id(0) == 0)
    def _():
        grad_ref[...] = sum_ref[:CHUNK, :].astype(f32)

    extra = sum_ref[CHUNK:, :].astype(f32)
    first = extra[0:8] + extra[8:16] + extra[16:24]
    loss = extra[24:32] + extra[32:40] + extra[40:48]
    total = jnp.broadcast_to(jnp.sum(first, axis=0, keepdims=True), (16, D))
    loss_ref[...] = jnp.broadcast_to(jnp.sum(loss, axis=0, keepdims=True), (8, D))
    stacked = jnp.concatenate(split3(total), axis=0)
    three = dot(stacked, p_ref[...])
    center_ref[...] = (three[0:1] + three[16:17] + three[32:33]) * (1.0 / TOTAL)


def finish(summed, prototypes):
    width = prototypes.shape[1]
    block = 2048
    return pl.pallas_call(
        finish_kernel,
        grid=(width // block,),
        in_specs=[
            pl.BlockSpec((CHUNK + EXTRA, D), lambda i: (0, 0)),
            pl.BlockSpec((D, block), lambda i: (0, i)),
        ],
        out_specs=[
            pl.BlockSpec((CHUNK, D), lambda i: (0, 0)),
            pl.BlockSpec((1, block), lambda i: (0, i)),
            pl.BlockSpec((8, D), lambda i: (0, 0)),
        ],
        out_shape=[
            jax.ShapeDtypeStruct((CHUNK, D), f32),
            jax.ShapeDtypeStruct((1, width), f32),
            jax.ShapeDtypeStruct((8, D), f32),
        ],
        compiler_params=params(),
        cost_estimate=cost(6 * 8 * D * width, 5 << 20),
    )(summed, prototypes)


def final_kernel(count_ref, index_ref, s_ref, du_ref, out_ref):
    for i in range(LOCAL):
        pick = picks(index_ref, count_ref[i], i)
        unit, length = unit_rows(dot(pick, s_ref[i], TN))
        d_unit = du_ref[:, i * SLOTS : (i + 1) * SLOTS].astype(f32).T
        row = (d_unit - unit * jnp.sum(unit * d_unit, axis=1, keepdims=True)) / length
        top = row.astype(bf16)
        rest = (row - top.astype(f32)).astype(bf16)
        out_ref[i] = dot(pick, top) + dot(pick, rest)


def shards(student_rows, teacher_rows, prototypes, center, mask_index, mask_count, loss_scale):
    z, core, x, y = (lax.axis_index(a) for a in ("z", "core", "x", "y"))
    ids = jnp.stack([z, core, x, y]).astype(jnp.int32)
    peers = ("core", "x", "y")

    mine = prep(mask_count, mask_index, student_rows, teacher_rows)
    other = lax.ppermute(mine, "core", [(0, 1), (1, 0)])
    stats, row_sum, turned, shifts = local_stats(ids, prototypes, center, mine, other)
    stats = lax.all_to_all(stats, peers, 0, 0)
    coef, misc = small_call(
        merge_kernel,
        [jax.ShapeDtypeStruct((8, BOTH), f32), jax.ShapeDtypeStruct((EXTRA, D), bf16)],
        ids, loss_scale.reshape(1), stats, mine, other, row_sum,
        smem=(0, 1),
    )
    parts, send = grads(ids, turned, shifts, prototypes, mine, other, coef, misc)
    summed = lax.psum_scatter(parts.reshape(-1, D), "z", scatter_dimension=0, tiled=True)
    proto_grad, patch_center, loss = finish(summed, prototypes)

    part = D // (X * Y)
    got = lax.all_to_all(send.reshape(PEERS, part, ROWS), peers, 0, 0)
    own = small_call(du_sum_kernel, jax.ShapeDtypeStruct((X * Y, part, ROWS), bf16), got)
    du = lax.all_to_all(own, ("x", "y"), 0, 0).reshape(D, ROWS)
    student_grad = small_call(
        final_kernel,
        jax.ShapeDtypeStruct(student_rows.shape, f32),
        mask_count, mask_index, student_rows, du,
        smem=(0,),
    )
    return (loss[0, 0], student_grad, proto_grad, patch_center.reshape(-1))


def solution(mesh):
    fine = Mesh(mesh.devices.reshape(Z, CORES, X, Y), ("z", "core", "x", "y"))
    dp, proto = ("z", "core"), ("x", "y")
    in_specs = (
        P(dp, None, None),
        P(dp, None, None),
        P(None, proto),
        P(proto),
        P(dp, None),
        P(dp),
        P(),
    )
    out_specs = (P(), P(dp, None, None), P(proto + dp, None), P(proto))
    return jax.shard_map(shards, mesh=fine, in_specs=in_specs, out_specs=out_specs, check_vma=False)
```

time: 116 us -> 126 us (1.086)
  starting transfers between devices: 31.8 us -> 7.83 us
  blocking collectives: 14 us -> 27.3 us
  between operations: 1.52 us -> 14.7 us
  Pallas kernels: 44.1 us -> 31.6 us
  waiting for transfers between devices: 14.6 us -> 25.9 us
  local copies, waits for them, and re-layouts: 9.76 us -> 18 us
    ppermute x16 -> x1, starting transfers between devices: 25.3 us -> 0.09 us  [shards(): other = lax.ppermute(mine, 'core', [(0, 1), (1, 0)])]
    all_to_all x0 -> x1, blocking collectives: none -> 15.4 us  [shards(): got = lax.all_to_all(send.reshape(PEERS, part, ROWS), peers, 0, 0)]
    reduce_scatter x0 -> x1, waiting for transfers between devices: none -> 13.2 us  [shards(): lax.psum_scatter(parts.reshape(-1, D), 'z', scatter_dimension=0, tiled=True)]
    ppermute x16 -> x1, waiting for transfers between devices: 14.6 us -> 1.84 us  [shards(): other = lax.ppermute(mine, 'core', [(0, 1), (1, 0)])]
    all_to_all x1, waiting for transfers between devices: 0.01 us -> 10.8 us  [shards(): stats = lax.all_to_all(stats, peers, 0, 0)]
    unnamed x34 -> x32, local copies, waits for them, and re-layouts: 8.52 us -> 17.5 us
    pallas_call x5 -> x3, Pallas kernels: 33.7 us -> 25.5 us  [the longest x1 12.6 us: local_stats(): pl.pallas_call(stats_kernel, in_specs=[smem, vmem, vmem, vmem, vmem], out...]
    pallas_call x12 -> x3, Pallas kernels: 7.99 us -> 3.66 us  [small_call(): pl.pallas_call(kernel, out_shape=out_shape, in_specs=specs, out_specs=jax...]
  transfers between devices with their start and end apart: 17 -> 3, of which waited for: 8 -> 3; matrix products, arithmetic and copies ran while one was open for 1% -> 0% of each run, Pallas kernels for 20% -> 2%
where the time goes in v3:
time: 126 us; the launch traced here: 125 us
  Pallas kernels  31.6 us (25%)
  blocking collectives  27.3 us (22%)
  waiting for transfers between devices  25.9 us (21%)
  local copies, waits for them, and re-layouts  18 us (14%)
  between operations  14.7 us (12%)
  starting transfers between devices  7.83 us (6%)
    unnamed x32, local copies, waits for them, and re-layouts  17.5 us
    all_to_all x1, blocking collectives, shards(): got = lax.all_to_all(send.reshape(PEERS, part, ROWS), peers, 0, 0)  15.4 us
    reduce_scatter x1, waiting for transfers between devices, shards(): lax.psum_scatter(parts.reshape(-1, D), 'z', scatter_dimension=0, tiled=True)  13.2 us
    pallas_call x1, Pallas kernels, local_stats(): pl.pallas_call(stats_kernel, in_specs=[smem, vmem, vmem, vmem, vmem], out...  12.6 us
    all_to_all x1, blocking collectives, shards(): du = lax.all_to_all(own, ('x', 'y'), 0, 0).reshape(D, ROWS)  11.9 us
    pallas_call x1, Pallas kernels, grads(): pl.pallas_call(grad_kernel, in_specs=[smem] + [vmem] * 7, out_specs=[vmem...  11.9 us
    all_to_all x1, waiting for transfers between devices, shards(): stats = lax.all_to_all(stats, peers, 0, 0)  10.8 us
    all_to_all x1, starting transfers between devices, shards(): stats = lax.all_to_all(stats, peers, 0, 0)  7.52 us
  transfers between devices with their start and end apart: 3, of which 3 were waited for; matrix products, arithmetic and copies ran while one was open for 0% of the time, Pallas kernels for 2%

profile of v3, /device:TPU:8, one launch (start us, length us, event | category | flops | bytes accessed | tf_op | source)
XLA Modules:
  0.0 125.5 jit_solution(8629826200418655066)
XLA Ops:
  7.2 0.0 copy-start.3
  7.2 1.0 copy-done.3
  8.2 0.0 copy-start.5
  8.2 1.0 copy-done.5
  9.3 0.0 copy-start.7
  9.3 0.7 copy-done.7
  9.9 0.0 copy-start.9
  9.9 0.7 copy-done.9
  10.6 1.1 shard_map.102.mine_ref
  11.7 0.1 collective-permute-start
  11.8 0.1 pad_add_fusion.ids_ref
  11.9 1.8 %collective-permute-done.other_ref = bf16[2,528,256]{2,1,0:T(8,128)(2,1)S(1)} collective-permute-done((bf16[2,528,256]{2,1,0:T(8,128)(2,1)S(1)}, bf16[2,528,256]{2,1,0:T(8,128)(2,1)S(1)}, u32[]{:S(2)}, u32[]{:S(2)}) %collective-permute-start) | collective-permute-done | bytes 540704 | tf_op jit(solution)/shard_map/ppermute | solution.py:351
  13.7 0.0 copy-start
  13.7 2.2 %copy-done = bf16[256,8192]{1,0:T(8,128)(2,1)S(1)} copy-done((bf16[256,8192]{1,0:T(8,128)(2,1)S(1)}, bf16[256,8192]{1,0:T(8,128)(2,1)}, u32[]{:S(2)}) %copy-start) | copy-done | bytes 4194328
  15.9 0.0 copy-start.11
  15.9 0.8 copy-done.11
  16.6 12.6 %shard_map.103 = (f32[32,40,128]{2,1,0:T(8,128)}, f32[8,256]{1,0:T(8,128)S(1)}, bf16[8,512,256]{2,1,0:T(8,128)(2,1)S(1)}, f32[8,512,128]{2,1,0:T(8,128)S(1)}) custom-call(s32[4]{0:T(128)S(1)} %pad_add_fusion.ids_ref, bf16[256,8192]{1,0:T(8,128)(2,1)S(1)} %copy-done, f32[1,8192]{1,0:T(1,128)S(1)} %bitcast.14, bf16[2,528,256]{2,1,0:T(8,128)(2,1)S(1)} %shard_map.102.mine_ref, ...), custom_call_target="tpu_custom_call" | custom-call | flops 4294967296 | bytes 6291456 | tf_op jit(solution)/shard_map/pallas_call | solution.py:152
  29.2 0.0 copy-start.12
  29.2 1.3 %copy-done.12 = bf16[8,512,256]{2,1,0:T(8,128)(2,1)} copy-done((bf16[8,512,256]{2,1,0:T(8,128)(2,1)}, bf16[8,512,256]{2,1,0:T(8,128)(2,1)S(1)}, u32[]{:S(2)}) %copy-start.12) | copy-done | bytes 2097176
  30.6 0.0 copy-start.14
  30.6 1.3 %copy-done.14 = f32[8,512,128]{2,1,0:T(8,128)} copy-done((f32[8,512,128]{2,1,0:T(8,128)}, f32[8,512,128]{2,1,0:T(8,128)S(1)}, u32[]{:S(2)}) %copy-start.14) | copy-done | bytes 2097176
  31.9 7.5 %all-to-all-start = ((f32[32,40,128]{2,1,0:T(8,128)}), f32[32,40,128]{2,1,0:T(8,128)S(1)}, u32[]{:S(2)}, u32[]{:S(2)}) async-start(f32[32,40,128]{2,1,0:T(8,128)} %get-tuple-element.17), calls=%async_computation | async-start | bytes 1310720 | tf_op jit(solution)/shard_map/all_to_all | solution.py:353
  39.4 0.2 reduce-scatter.2.cloned.1.call-start
  40.3 10.8 %all-to-all-done.got_ref = f32[32,40,128]{2,1,0:T(8,128)S(1)} async-done(((f32[32,40,128]{2,1,0:T(8,128)}), f32[32,40,128]{2,1,0:T(8,128)S(1)}, u32[]{:S(2)}, u32[]{:S(2)}) %all-to-all-start) | async-done | bytes 655392 | tf_op jit(solution)/shard_map/all_to_all | solution.py:353
  51.1 0.7 shard_map.104
  51.8 0.0 copy-start.1
  51.8 2.2 %copy-done.1 = bf16[256,8192]{1,0:T(8,128)(2,1)S(1)} copy-done((bf16[256,8192]{1,0:T(8,128)(2,1)S(1)}, bf16[256,8192]{1,0:T(8,128)(2,1)}, u32[]{:S(2)}) %copy-start.1) | copy-done | bytes 4194328
  54.0 0.0 copy-start.13
  54.0 1.6 %copy-done.13 = bf16[8,512,256]{2,1,0:T(8,128)(2,1)S(1)} copy-done((bf16[8,512,256]{2,1,0:T(8,128)(2,1)S(1)}, bf16[8,512,256]{2,1,0:T(8,128)(2,1)}, u32[]{:S(2)}) %copy-start.13) | copy-done | bytes 2097176
  55.6 0.0 copy-start.15
  55.6 1.6 %copy-done.15 = f32[8,512,128]{2,1,0:T(8,128)S(1)} copy-done((f32[8,512,128]{2,1,0:T(8,128)S(1)}, f32[8,512,128]{2,1,0:T(8,128)}, u32[]{:S(2)}) %copy-start.15) | copy-done | bytes 2097176
  57.2 11.9 %shard_map.105 = (bf16[8,560,256]{2,1,0:T(8,128)(2,1)}, bf16[2,256,512]{2,1,0:T(8,128)(2,1)S(1)}) custom-call(s32[4]{0:T(128)S(1)} %pad_add_fusion.ids_ref, bf16[8,512,256]{2,1,0:T(8,128)(2,1)S(1)} %copy-done.13, f32[8,512,128]{2,1,0:T(8,128)S(1)} %copy-done.15, bf16[256,8192]{1,0:T(8,128)(2,1)S(1)} %copy-done.1, ...), custom_call_target="tpu_custom_call" | custom-call | flops 8589934592 | bytes 8388608 | tf_op jit(solution)/shard_map/pallas_call | solution.py:275
  69.0 0.0 copy-start.4
  69.0 0.0 copy-start.8
  69.0 0.0 copy-start.10
  69.0 0.0 reduce-scatter.2.cloned.1.call-update
  69.1 15.4 %all_to_all.15.got_ref = bf16[32,16,512]{2,1,0:T(8,128)(2,1)S(1)} all-to-all(bf16[32,16,512]{2,1,0:T(8,128)(2,1)S(1)} %bitcast.13), channel_id=1, replica_groups=mesh['z'=8,'core'=2,'x'=4,'y'=4] {'core','x','y'}, dimensions={0} | all-to-all | bytes 1048576 | tf_op jit(solution)/shard_map/all_to_all | solution.py:365
  84.5 0.1 shard_map.107
  84.6 11.9 %all_to_all.16 = bf16[16,16,512]{2,1,0:T(8,128)(2,1)S(1)} all-to-all(bf16[16,16,512]{2,1,0:T(8,128)(2,1)S(1)} %shard_map.107), channel_id=1, replica_groups=mesh['z'=8,'core'=2,'x'=4,'y'=4] {'x','y'}, dimensions={0} | all-to-all | bytes 524288 | tf_op jit(solution)/shard_map/all_to_all | solution.py:367
  96.5 0.0 copy-done.4
  96.5 0.0 copy-done.8
  96.5 0.0 copy-done.10
  96.5 2.9 %shard_map.108 = f32[4,256,256]{2,1,0:T(8,128)} custom-call(s32[4]{0:T(128)S(1)} %copy-done.10, s32[4,128]{1,0:T(4,128)S(1)} %copy-done.8, bf16[4,256,256]{2,1,0:T(8,128)(2,1)S(1)} %copy-done.4, bf16[256,512]{1,0:T(8,128)(2,1)S(1)} %bitcast.12), custom_call_target="tpu_custom_call" | custom-call | flops 1048576 | bytes 262144 | tf_op jit(solution)/shard_map/pallas_call | solution.py:234
  99.3 13.2 %reduce-scatter.2.cloned.1.call-done.sum_ref = bf16[560,256]{1,0:T(8,128)(2,1)} async-done(((bf16[4480,256]{1,0:T(8,128)(2,1)}), bf16[560,256]{1,0:T(8,128)(2,1)}) %reduce-scatter.2.cloned.1.call-update) | async-done | bytes 286736 | tf_op jit(solution)/shard_map/reduce_scatter | solution.py:361
  112.6 0.0 copy-start.2
  112.6 2.2 %copy-done.2 = bf16[256,8192]{1,0:T(8,128)(2,1)S(1)} copy-done((bf16[256,8192]{1,0:T(8,128)(2,1)S(1)}, bf16[256,8192]{1,0:T(8,128)(2,1)}, u32[]{:S(2)}) %copy-start.2) | copy-done | bytes 4194328
  114.8 0.0 copy-start.6
  114.8 1.0 copy-done.6
  115.7 2.4 %shard_map.106 = (f32[512,256]{1,0:T(8,128)}, f32[1,8192]{1,0:T(1,128)}, f32[8,256]{1,0:T(8,128)S(1)}) custom-call(bf16[560,256]{1,0:T(8,128)(2,1)S(1)} %copy-done.6, bf16[256,8192]{1,0:T(8,128)(2,1)S(1)} %copy-done.2), custom_call_target="tpu_custom_call" | custom-call | flops 100663296 | bytes 5242880 | tf_op jit(solution)/shard_map/pallas_call | solution.py:312
  118.1 0.5 slice.3
Async XLA Ops:
  7.2 1.0 copy-start.3
  8.2 1.0 copy-start.5
  9.3 0.7 copy-start.7
  9.9 0.7 copy-start.9
  11.7 2.0 %collective-permute-start = (bf16[2,528,256]{2,1,0:T(8,128)(2,1)S(1)}, bf16[2,528,256]{2,1,0:T(8,128)(2,1)S(1)}, u32[]{:S(2)}, u32[]{:S(2)}) collective-permute-start(bf16[2,528,256]{2,1,0:T(8,128)(2,1)S(1)} %shard_map.102.mine_ref), channel_id=1, source_target_pairs={{0,16},{16,0},{1,17},{17,1},{2,18},{18,2},{3,19},{19,3},{4,20},{20... | collective-permute-start | bytes 1622024 | tf_op jit(solution)/shard_map/ppermute | solution.py:351
  13.7 2.2 %copy-start = (bf16[256,8192]{1,0:T(8,128)(2,1)S(1)}, bf16[256,8192]{1,0:T(8,128)(2,1)}, u32[]{:S(2)}) copy-start(bf16[256,8192]{1,0:T(8,128)(2,1)} %p_ref.5) | copy-start | bytes 12582916
  15.9 0.8 copy-start.11
  29.2 1.3 %copy-start.12 = (bf16[8,512,256]{2,1,0:T(8,128)(2,1)}, bf16[8,512,256]{2,1,0:T(8,128)(2,1)S(1)}, u32[]{:S(2)}) copy-start(bf16[8,512,256]{2,1,0:T(8,128)(2,1)S(1)} %get-tuple-element.15.pt_ref) | copy-start | bytes 6291460
  30.6 1.3 %copy-start.14 = (f32[8,512,128]{2,1,0:T(8,128)}, f32[8,512,128]{2,1,0:T(8,128)S(1)}, u32[]{:S(2)}) copy-start(f32[8,512,128]{2,1,0:T(8,128)S(1)} %get-tuple-element.16.cb_ref) | copy-start | bytes 6291460
  31.9 19.2 %all-to-all-start = ((f32[32,40,128]{2,1,0:T(8,128)}), f32[32,40,128]{2,1,0:T(8,128)S(1)}, u32[]{:S(2)}, u32[]{:S(2)}) async-start(f32[32,40,128]{2,1,0:T(8,128)} %get-tuple-element.17), calls=%async_computation | async-start | bytes 1310720 | tf_op jit(solution)/shard_map/all_to_all | solution.py:353
  39.4 73.2 %reduce-scatter.2.cloned.1.call-start = ((), (), s32[]{:S(2)}) async-start(), calls=%async_computation.4 | async-start | bytes 2580480 | tf_op jit(solution)/shard_map/reduce_scatter | solution.py:361
  51.8 2.2 %copy-start.1 = (bf16[256,8192]{1,0:T(8,128)(2,1)S(1)}, bf16[256,8192]{1,0:T(8,128)(2,1)}, u32[]{:S(2)}) copy-start(bf16[256,8192]{1,0:T(8,128)(2,1)} %p_ref.5) | copy-start | bytes 12582916
  54.0 1.6 %copy-start.13 = (bf16[8,512,256]{2,1,0:T(8,128)(2,1)S(1)}, bf16[8,512,256]{2,1,0:T(8,128)(2,1)}, u32[]{:S(2)}) copy-start(bf16[8,512,256]{2,1,0:T(8,128)(2,1)} %copy-done.12) | copy-start | bytes 6291460
  55.6 1.6 %copy-start.15 = (f32[8,512,128]{2,1,0:T(8,128)S(1)}, f32[8,512,128]{2,1,0:T(8,128)}, u32[]{:S(2)}) copy-start(f32[8,512,128]{2,1,0:T(8,128)} %copy-done.14) | copy-start | bytes 6291460
  69.0 27.4 %copy-start.4 = (bf16[4,256,256]{2,1,0:T(8,128)(2,1)S(1)}, bf16[4,256,256]{2,1,0:T(8,128)(2,1)}, u32[]{:S(2)}) copy-start(bf16[4,256,256]{2,1,0:T(8,128)(2,1)} %s_ref.3) | copy-start | bytes 1572868
  69.0 27.4 %copy-start.8 = (s32[4,128]{1,0:T(4,128)S(1)}, s32[4,128]{1,0:T(4,128)}, u32[]{:S(2)}) copy-start(s32[4,128]{1,0:T(4,128)} %index_ref.3) | copy-start | bytes 6148
  69.0 27.4 %copy-start.10 = (s32[4]{0:T(128)S(1)}, s32[4]{0:T(128)}, u32[]{:S(2)}) copy-start(s32[4]{0:T(128)} %count_ref.3) | copy-start | bytes 52
  112.6 2.2 %copy-start.2 = (bf16[256,8192]{1,0:T(8,128)(2,1)S(1)}, bf16[256,8192]{1,0:T(8,128)(2,1)}, u32[]{:S(2)}) copy-start(bf16[256,8192]{1,0:T(8,128)(2,1)} %p_ref.5) | copy-start | bytes 12582916
  114.8 1.0 copy-start.6
Sparse Core Ops, SparseCore 0:
  69.2 43.3 reduce-scatter.1
